TPU v7x, 512 devices: a whole 4x4x16 slice. The times are simulated.
512 devices in a mesh: gx: 64 (over z, x_lo, core), gy: 8 (over y, x_hi).
Axes of the slice: x: 4 (x_hi: 2, x_lo: 2; x = x_hi * 2 + x_lo), y: 4, z: 16, core: 2. Of those that a mesh axis runs over, the one named last changes fastest.
Arguments:
- grad_late: float32 [2, 20, 512, 1024], P(None, None, 'gx', 'gy'), may hold values from -6 to 6
- grad_early: float32 [2, 20, 512, 1024], P(None, None, 'gx', 'gy'), may hold values from -6 to 6
- accumulation: bfloat16 [4, 20, 512, 1024], P(None, None, 'gx', 'gy'), may hold values from -0.021 to 0.302, as said below
- mobility_late: bfloat16 [4, 20, 512, 1024], P(None, None, 'gx', 'gy'), may hold values from -0.25 to 1.4, as said below
- mobility_early: bfloat16 [4, 20, 512, 1024], P(None, None, 'gx', 'gy'), may hold values from -0.25 to 1.4, as said below
- trans_x: bfloat16 [20, 512, 1024], P(None, 'gx', 'gy'), may hold values from 0.0099487305 to 1
- trans_y: bfloat16 [20, 512, 1024], P(None, 'gx', 'gy'), may hold values from 0.0099487305 to 1
- trans_z: bfloat16 [20, 512, 1024], P(None, 'gx', 'gy'), may hold values from 0.0099487305 to 1
- perf_cell: int32 [64, 8, 256], P('gx', 'gy'), may hold values from 0 to 20479
- perf_well: int32 [64, 8, 256], P('gx', 'gy'), may hold values from 0 to 511
- productivity: float32 [64, 8, 256], P('gx', 'gy'), may hold values from 0.3 to 3
Outputs:
- adjoint_early: float32 [2, 20, 512, 1024], P(None, None, 'gx', 'gy')
- well_partials: float32 [4, 512], P(None, 'gx')
Inputs may be any that keep to these rules, and one draw needn't show every extreme that they name: `accumulation`: off-diagonal entries c1, c2 lie within 0.021 in magnitude, diagonal entries c0, c3 from 0.05 to 0.302. `mobility_late`: off-diagonal entries b1, b2 lie within 0.25 in magnitude, diagonal entries b0, b3 from 0.6 to 1.4. `mobility_early`: off-diagonal entries b1, b2 lie within 0.25 in magnitude, diagonal entries b0, b3 from 0.6 to 1.4.
All inputs are finite; a program needn't handle non-finite values.
Results may differ from a plain program's by a relative error of at most 0.0003.
Values may be sent and summed in bfloat16 or wider, within the bound.
A program may use at most 64 MiB of HBM per device.

v0:
```python
import jax
import jax.numpy as jnp
from jax import lax
from jax.sharding import PartitionSpec as P

SWEEPS = 3
WELL_DEV = 8


def shifted(block, axis, distance):
    devices = range(lax.axis_size(axis))
    route = [(i - distance, i) for i in devices if i - distance in devices]
    return lax.ppermute(block, axis, route)


def extended(cells, sides, width):
    for axis, dim in sides:
        count = lax.axis_size(axis)
        ends = count - 1
        head = lax.slice_in_dim(cells, 0, width, axis=dim)
        tail = lax.slice_in_dim(cells, cells.shape[dim] - width, cells.shape[dim], axis=dim)
        cells = jnp.concatenate(
            [
                lax.ppermute(tail, axis, [(i, (i + 1) % count) for i in range(ends)]),
                cells,
                lax.ppermute(head, axis, [((i + 1) % count, i) for i in range(ends)]),
            ],
            axis=dim,
        )
    return cells


def transpose_apply(matrix, vector):
    return jnp.stack(
        [
            matrix[0] * vector[0] + matrix[2] * vector[1],
            matrix[1] * vector[0] + matrix[3] * vector[1],
        ]
    )


def face_total(padded_x, padded_y, layer_trans):
    upper_trans = jnp.concatenate([layer_trans[1:], jnp.zeros_like(layer_trans[:1])], 0)
    return (
        padded_x[:, 1:-1, 1:-1]
        + padded_x[:, 2:, 1:-1]
        + padded_y[:, 1:-1, 1:-1]
        + padded_y[:, 1:-1, 2:]
        + layer_trans
        + upper_trans
    )


def diag_inverse(padded_x, padded_y, layer_trans, accum_full, mobility, inside):
    facesum = face_total(padded_x, padded_y, layer_trans)
    diag_block = accum_full + facesum[None] * mobility
    determinant = diag_block[0] * diag_block[3] - diag_block[1] * diag_block[2]
    determinant = jnp.where(inside > 0, determinant, jnp.float32(1.0))
    det_scale = inside / determinant
    return jnp.stack(
        [
            diag_block[3] * det_scale,
            -diag_block[1] * det_scale,
            -diag_block[2] * det_scale,
            diag_block[0] * det_scale,
        ]
    )


def jacobi_sweep(adjoint_pad, padded_x, padded_y, layer_trans, source, mobility, inverse):
    centre = adjoint_pad[:, :, 1:-1, 1:-1]
    inflow = (
        padded_x[None, :, 1:-1, 1:-1] * adjoint_pad[:, :, :-2, 1:-1]
        + padded_x[None, :, 2:, 1:-1] * adjoint_pad[:, :, 2:, 1:-1]
    )
    inflow = (
        inflow
        + padded_y[None, :, 1:-1, 1:-1] * adjoint_pad[:, :, 1:-1, :-2]
        + padded_y[None, :, 1:-1, 2:] * adjoint_pad[:, :, 1:-1, 2:]
    )
    zero_layer = jnp.zeros_like(centre[:, :1])
    lower_cell = jnp.concatenate([zero_layer, centre[:, :-1]], 1)
    upper_cell = jnp.concatenate([centre[:, 1:], zero_layer], 1)
    upper_trans = jnp.concatenate([layer_trans[1:], jnp.zeros_like(layer_trans[:1])], 0)
    inflow = inflow + layer_trans[None] * lower_cell + upper_trans[None] * upper_cell
    return transpose_apply(inverse, source + transpose_apply(mobility, inflow))


def per_device(
    grad_late,
    grad_early,
    accumulation,
    mobility_late,
    mobility_early,
    trans_x,
    trans_y,
    trans_z,
    perf_cell,
    perf_well,
    productivity,
):
    layers, rows, columns = trans_x.shape
    row_ids = lax.axis_index("gx") * rows + jnp.arange(rows)
    col_ids = lax.axis_index("gy") * columns + jnp.arange(columns)
    layer_ids = jnp.arange(layers)
    masked_x = trans_x.astype(jnp.float32) * (row_ids > 0).astype(jnp.float32)[None, :, None]
    masked_y = trans_y.astype(jnp.float32) * (col_ids > 0).astype(jnp.float32)[None, None, :]
    masked_z = trans_z.astype(jnp.float32) * (layer_ids > 0).astype(jnp.float32)[:, None, None]
    above_x = shifted(masked_x[:, :1, :].astype(jnp.bfloat16), "gx", -1).astype(jnp.float32)
    above_y = shifted(masked_y[:, :, :1].astype(jnp.bfloat16), "gy", -1).astype(jnp.float32)
    padded_x = jnp.concatenate([jnp.zeros_like(above_x), masked_x, above_x], 1)
    padded_x = jnp.pad(padded_x, ((0, 0), (0, 0), (1, 1)))
    padded_y = jnp.concatenate([jnp.zeros_like(above_y), masked_y, above_y], 2)
    padded_y = jnp.pad(padded_y, ((0, 0), (1, 1), (0, 0)))
    inside = jnp.ones((layers, rows, columns), jnp.float32)
    accum_full = accumulation.astype(jnp.float32)

    def solve(source, mobility_arg):
        mobility = mobility_arg.astype(jnp.float32)
        inverse = diag_inverse(padded_x, padded_y, masked_z, accum_full, mobility, inside)
        adjoint = transpose_apply(inverse, source)
        for sweep_index in range(SWEEPS):
            adjoint_pad = extended(adjoint, (("gx", 2), ("gy", 3)), 1)
            adjoint = jacobi_sweep(
                adjoint_pad, padded_x, padded_y, masked_z, source, mobility, inverse
            )
        return adjoint

    adjoint_late = solve(grad_late, mobility_late)
    adjoint_early = solve(grad_early + transpose_apply(accum_full, adjoint_late), mobility_early)
    values = jnp.concatenate([adjoint_early, adjoint_late], 0).reshape(4, -1)
    cell_ids = perf_cell.reshape(-1)
    well_ids = perf_well.reshape(-1)
    picked = jnp.take(values, cell_ids, axis=1) * productivity.reshape(-1)[None]
    nwells = WELL_DEV * lax.axis_size("gx")
    onehot = (well_ids[:, None] == jnp.arange(nwells)[None, :]).astype(jnp.float32)
    partial_value = jnp.dot(
        picked, onehot, precision=lax.Precision.HIGHEST, preferred_element_type=jnp.float32
    )
    owned = lax.psum_scatter(partial_value, "gx", scatter_dimension=1, tiled=True)
    well_partials = lax.psum(owned, "gy")
    return (adjoint_early, well_partials)


def solution(mesh):
    return jax.shard_map(
        per_device,
        mesh=mesh,
        in_specs=(
            P(None, None, "gx", "gy"),
            P(None, None, "gx", "gy"),
            P(None, None, "gx", "gy"),
            P(None, None, "gx", "gy"),
            P(None, None, "gx", "gy"),
            P(None, "gx", "gy"),
            P(None, "gx", "gy"),
            P(None, "gx", "gy"),
            P("gx", "gy", None),
            P("gx", "gy", None),
            P("gx", "gy", None),
        ),
        out_specs=(P(None, None, "gx", "gy"), P(None, "gx")),
        check_vma=False,
    )
```

profile of v0, /device:TPU:128, one launch (start us, length us, event | category | flops | bytes accessed | tf_op | source)
XLA Modules:
  0.0 320.5 jit_solution(5821516998994916361)
XLA Ops:
  3.0 2.4 collective-permute-start
  6.2 2.8 collective-permute-done.1
  13.2 1.9 collective-permute-start.2
  15.2 5.9 %collective-permute-start.3 = (f32[2,20,1,128]{3,2,1,0:T(1,128)S(1)}, f32[2,20,1,128]{3,2,1,0:T(1,128)S(1)}, u32[]{:S(2)}, u32[]{:S(2)}) collective-permute-start(f32[2,20,1,128]{3,2,1,0:T(1,128)S(1)} %get-tuple-element.68), channel_id=1, source_target_pairs={{8,0},{16,8},{24,16},{32,24},{40,32},{48,40},{56,48},{64,56},{72,6... | collective-permute-start | bytes 61448 | tf_op jit(solution)/shard_map/ppermute | solution.py:26
  22.7 5.8 %collective-permute-start.4 = (f32[2,20,10,1]{3,2,1,0:T(8,128)S(1)}, f32[2,20,10,1]{3,2,1,0:T(8,128)S(1)}, u32[]{:S(2)}, u32[]{:S(2)}) collective-permute-start(f32[2,20,10,1]{3,2,1,0:T(8,128)S(1)} %get-tuple-element.43), channel_id=1, source_target_pairs={{0,1},{1,2},{2,3},{3,4},{4,5},{5,6},{6,7},{8,9},{9,10},{10,11},{11... | collective-permute-start | bytes 4808 | tf_op jit(solution)/shard_map/ppermute | solution.py:24
  29.9 5.0 %collective-permute-done.4 = f32[2,20,10,1]{3,2,1,0:T(8,128)S(1)} collective-permute-done((f32[2,20,10,1]{3,2,1,0:T(8,128)S(1)}, f32[2,20,10,1]{3,2,1,0:T(8,128)S(1)}, u32[]{:S(2)}, u32[]{:S(2)}) %collective-permute-start.4) | collective-permute-done | bytes 1632 | tf_op jit(solution)/shard_map/ppermute | solution.py:24
  34.9 9.3 %collective-permute-done.5 = f32[2,20,10,1]{3,2,1,0:T(8,128)S(1)} collective-permute-done((f32[2,20,10,1]{3,2,1,0:T(8,128)S(1)}, f32[2,20,10,1]{3,2,1,0:T(8,128)S(1)}, u32[]{:S(2)}, u32[]{:S(2)}) %collective-permute-start.5) | collective-permute-done | bytes 1632 | tf_op jit(solution)/shard_map/ppermute | solution.py:26
  47.5 5.8 %collective-permute-start.7 = (f32[2,20,1,128]{3,2,1,0:T(1,128)S(1)}, f32[2,20,1,128]{3,2,1,0:T(1,128)S(1)}, u32[]{:S(2)}, u32[]{:S(2)}) collective-permute-start(f32[2,20,1,128]{3,2,1,0:T(1,128)S(1)} %get-tuple-element.64), channel_id=1, source_target_pairs={{8,0},{16,8},{24,16},{32,24},{40,32},{48,40},{56,48},{64,56},{72,6... | collective-permute-start | bytes 61448 | tf_op jit(solution)/shard_map/ppermute | solution.py:26
  54.9 4.6 %collective-permute-start.8 = (f32[2,20,10,1]{3,2,1,0:T(8,128)S(1)}, f32[2,20,10,1]{3,2,1,0:T(8,128)S(1)}, u32[]{:S(2)}, u32[]{:S(2)}) collective-permute-start(f32[2,20,10,1]{3,2,1,0:T(8,128)S(1)} %get-tuple-element.41), channel_id=1, source_target_pairs={{0,1},{1,2},{2,3},{3,4},{4,5},{5,6},{6,7},{8,9},{9,10},{10,11},{11... | collective-permute-start | bytes 4808 | tf_op jit(solution)/shard_map/ppermute | solution.py:24
  60.9 3.2 %collective-permute-done.8 = f32[2,20,10,1]{3,2,1,0:T(8,128)S(1)} collective-permute-done((f32[2,20,10,1]{3,2,1,0:T(8,128)S(1)}, f32[2,20,10,1]{3,2,1,0:T(8,128)S(1)}, u32[]{:S(2)}, u32[]{:S(2)}) %collective-permute-start.8) | collective-permute-done | bytes 1632 | tf_op jit(solution)/shard_map/ppermute | solution.py:24
  64.1 9.3 %collective-permute-done.9 = f32[2,20,10,1]{3,2,1,0:T(8,128)S(1)} collective-permute-done((f32[2,20,10,1]{3,2,1,0:T(8,128)S(1)}, f32[2,20,10,1]{3,2,1,0:T(8,128)S(1)}, u32[]{:S(2)}, u32[]{:S(2)}) %collective-permute-start.9) | collective-permute-done | bytes 1632 | tf_op jit(solution)/shard_map/ppermute | solution.py:26
  75.8 5.8 %collective-permute-start.11 = (f32[2,20,1,128]{3,2,1,0:T(1,128)S(1)}, f32[2,20,1,128]{3,2,1,0:T(1,128)S(1)}, u32[]{:S(2)}, u32[]{:S(2)}) collective-permute-start(f32[2,20,1,128]{3,2,1,0:T(1,128)S(1)} %get-tuple-element.60), channel_id=1, source_target_pairs={{8,0},{16,8},{24,16},{32,24},{40,32},{48,40},{56,48},{64,56},{72,6... | collective-permute-start | bytes 61448 | tf_op jit(solution)/shard_map/ppermute | solution.py:26
  83.2 4.5 %collective-permute-start.12 = (f32[2,20,10,1]{3,2,1,0:T(8,128)S(1)}, f32[2,20,10,1]{3,2,1,0:T(8,128)S(1)}, u32[]{:S(2)}, u32[]{:S(2)}) collective-permute-start(f32[2,20,10,1]{3,2,1,0:T(8,128)S(1)} %get-tuple-element.39), channel_id=1, source_target_pairs={{0,1},{1,2},{2,3},{3,4},{4,5},{5,6},{6,7},{8,9},{9,10},{10,11},{11... | collective-permute-start | bytes 4808 | tf_op jit(solution)/shard_map/ppermute | solution.py:24
  89.0 4.4 %collective-permute-done.12 = f32[2,20,10,1]{3,2,1,0:T(8,128)S(1)} collective-permute-done((f32[2,20,10,1]{3,2,1,0:T(8,128)S(1)}, f32[2,20,10,1]{3,2,1,0:T(8,128)S(1)}, u32[]{:S(2)}, u32[]{:S(2)}) %collective-permute-start.12) | collective-permute-done | bytes 1632 | tf_op jit(solution)/shard_map/ppermute | solution.py:24
  93.4 9.3 %collective-permute-done.13 = f32[2,20,10,1]{3,2,1,0:T(8,128)S(1)} collective-permute-done((f32[2,20,10,1]{3,2,1,0:T(8,128)S(1)}, f32[2,20,10,1]{3,2,1,0:T(8,128)S(1)}, u32[]{:S(2)}, u32[]{:S(2)}) %collective-permute-start.13) | collective-permute-done | bytes 1632 | tf_op jit(solution)/shard_map/ppermute | solution.py:26
  103.4 1.9 collective-permute-start.14
  105.3 5.8 %collective-permute-start.15 = (f32[2,20,1,128]{3,2,1,0:T(1,128)S(1)}, f32[2,20,1,128]{3,2,1,0:T(1,128)S(1)}, u32[]{:S(2)}, u32[]{:S(2)}) collective-permute-start(f32[2,20,1,128]{3,2,1,0:T(1,128)S(1)} %get-tuple-element.58), channel_id=1, source_target_pairs={{8,0},{16,8},{24,16},{32,24},{40,32},{48,40},{56,48},{64,56},{72,6... | collective-permute-start | bytes 61448 | tf_op jit(solution)/shard_map/ppermute | solution.py:26
  112.7 3.8 %collective-permute-start.16 = (f32[2,20,10,1]{3,2,1,0:T(8,128)S(1)}, f32[2,20,10,1]{3,2,1,0:T(8,128)S(1)}, u32[]{:S(2)}, u32[]{:S(2)}) collective-permute-start(f32[2,20,10,1]{3,2,1,0:T(8,128)S(1)} %get-tuple-element.37), channel_id=1, source_target_pairs={{0,1},{1,2},{2,3},{3,4},{4,5},{5,6},{6,7},{8,9},{9,10},{10,11},{11... | collective-permute-start | bytes 4808 | tf_op jit(solution)/shard_map/ppermute | solution.py:24
  117.9 4.0 %collective-permute-done.16 = f32[2,20,10,1]{3,2,1,0:T(8,128)S(1)} collective-permute-done((f32[2,20,10,1]{3,2,1,0:T(8,128)S(1)}, f32[2,20,10,1]{3,2,1,0:T(8,128)S(1)}, u32[]{:S(2)}, u32[]{:S(2)}) %collective-permute-start.16) | collective-permute-done | bytes 1632 | tf_op jit(solution)/shard_map/ppermute | solution.py:24
  121.9 7.8 %collective-permute-done.17 = f32[2,20,10,1]{3,2,1,0:T(8,128)S(1)} collective-permute-done((f32[2,20,10,1]{3,2,1,0:T(8,128)S(1)}, f32[2,20,10,1]{3,2,1,0:T(8,128)S(1)}, u32[]{:S(2)}, u32[]{:S(2)}) %collective-permute-start.17) | collective-permute-done | bytes 1632 | tf_op jit(solution)/shard_map/ppermute | solution.py:26
  130.1 1.9 collective-permute-start.18
  132.0 5.8 %collective-permute-start.19 = (f32[2,20,1,128]{3,2,1,0:T(1,128)S(1)}, f32[2,20,1,128]{3,2,1,0:T(1,128)S(1)}, u32[]{:S(2)}, u32[]{:S(2)}) collective-permute-start(f32[2,20,1,128]{3,2,1,0:T(1,128)S(1)} %get-tuple-element.54), channel_id=1, source_target_pairs={{8,0},{16,8},{24,16},{32,24},{40,32},{48,40},{56,48},{64,56},{72,6... | collective-permute-start | bytes 61448 | tf_op jit(solution)/shard_map/ppermute | solution.py:26
  142.7 4.5 %collective-permute-done.20 = f32[2,20,10,1]{3,2,1,0:T(8,128)S(1)} collective-permute-done((f32[2,20,10,1]{3,2,1,0:T(8,128)S(1)}, f32[2,20,10,1]{3,2,1,0:T(8,128)S(1)}, u32[]{:S(2)}, u32[]{:S(2)}) %collective-permute-start.20) | collective-permute-done | bytes 1632 | tf_op jit(solution)/shard_map/ppermute | solution.py:24
  147.2 7.8 %collective-permute-done.21 = f32[2,20,10,1]{3,2,1,0:T(8,128)S(1)} collective-permute-done((f32[2,20,10,1]{3,2,1,0:T(8,128)S(1)}, f32[2,20,10,1]{3,2,1,0:T(8,128)S(1)}, u32[]{:S(2)}, u32[]{:S(2)}) %collective-permute-start.21) | collective-permute-done | bytes 1632 | tf_op jit(solution)/shard_map/ppermute | solution.py:26
  155.4 1.9 collective-permute-start.22
  157.3 5.8 %collective-permute-start.23 = (f32[2,20,1,128]{3,2,1,0:T(1,128)S(1)}, f32[2,20,1,128]{3,2,1,0:T(1,128)S(1)}, u32[]{:S(2)}, u32[]{:S(2)}) collective-permute-start(f32[2,20,1,128]{3,2,1,0:T(1,128)S(1)} %get-tuple-element.50), channel_id=1, source_target_pairs={{8,0},{16,8},{24,16},{32,24},{40,32},{48,40},{56,48},{64,56},{72,6... | collective-permute-start | bytes 61448 | tf_op jit(solution)/shard_map/ppermute | solution.py:26
  168.1 3.9 %collective-permute-done.24 = f32[2,20,10,1]{3,2,1,0:T(8,128)S(1)} collective-permute-done((f32[2,20,10,1]{3,2,1,0:T(8,128)S(1)}, f32[2,20,10,1]{3,2,1,0:T(8,128)S(1)}, u32[]{:S(2)}, u32[]{:S(2)}) %collective-permute-start.24) | collective-permute-done | bytes 1632 | tf_op jit(solution)/shard_map/ppermute | solution.py:24
  172.0 7.8 %collective-permute-done.25 = f32[2,20,10,1]{3,2,1,0:T(8,128)S(1)} collective-permute-done((f32[2,20,10,1]{3,2,1,0:T(8,128)S(1)}, f32[2,20,10,1]{3,2,1,0:T(8,128)S(1)}, u32[]{:S(2)}, u32[]{:S(2)}) %collective-permute-start.25) | collective-permute-done | bytes 1632 | tf_op jit(solution)/shard_map/ppermute | solution.py:26
  181.1 5.5 %copy.17 = f32[4,20480]{0,1:T(8,128)} copy(f32[4,20480]{1,0:T(4,128)S(1)} %pad_maximum_fusion.6) | data formatting | bytes 655360 | tf_op jit(solution)/shard_map/concatenate | solution.py:131
  186.7 4.7 %gather_fusion = f32[256,4]{1,0:T(8,128)S(1)} fusion(f32[4,20480]{0,1:T(8,128)} %copy.17, s32[1024]{0:T(1024)S(1)} %pad_clamp_fusion), kind=kCustom, calls=%fused_computation | custom fusion | bytes 9216 | tf_op jit(solution)/shard_map/jit(_take)/gather | solution.py:134
  191.8 108.2 %all-reduce.13 = f32[4,512]{1,0:T(4,128)S(1)} all-reduce(f32[4,512]{1,0:T(4,128)S(1)} %fusion), channel_id=2, replica_groups=mesh['gx'=64,'gy'=8] {'gx'}, use_global_device_ids=true, to_apply=%region_0.1.clone | all-reduce | flops 2048 | bytes 16384
  300.0 20.5 %psum.7 = f32[4,8]{1,0:T(4,128)} all-reduce(f32[4,8]{1,0:T(4,128)S(1)} %constant_dynamic-slice_fusion), channel_id=1, replica_groups=mesh['gx'=64,'gy'=8] {'gy'}, use_global_device_ids=true, to_apply=%region_1.2 | all-reduce | flops 32 | bytes 256 | tf_op jit(solution)/shard_map/psum | solution.py:141
  (115 shorter events, 37.1 us)
Async XLA Ops:
  0.6 80.9 %copy-start.2 = (bf16[4,20,8,128]{3,2,1,0:T(8,128)(2,1)S(1)}, bf16[4,20,8,128]{3,2,1,0:T(8,128)(2,1)}, u32[]{:S(2)}) copy-start(bf16[4,20,8,128]{3,2,1,0:T(8,128)(2,1)} %param.13) | copy-start | bytes 491524
  0.6 73.1 %copy-start = (f32[2,20,8,128]{3,2,1,0:T(8,128)S(1)}, f32[2,20,8,128]{3,2,1,0:T(8,128)}, u32[]{:S(2)}) copy-start(f32[2,20,8,128]{3,2,1,0:T(8,128)} %param.11) | copy-start | bytes 491524
  1.6 7.4 %collective-permute-start.1 = (bf16[20,8,1]{2,1,0:T(8,128)(2,1)S(1)}, bf16[20,8,1]{2,1,0:T(8,128)(2,1)S(1)}, u32[]{:S(2)}, u32[]{:S(2)}) collective-permute-start(bf16[20,8,1]{2,1,0:T(8,128)(2,1)S(1)} %slice.794), channel_id=1, source_target_pairs={{1,0},{2,1},{3,2},{4,3},{5,4},{6,5},{7,6},{9,8},{10,9},{11,10},{12... | collective-permute-start | bytes 968 | tf_op jit(solution)/shard_map/ppermute | solution.py:13
  3.0 6.1 %collective-permute-start = (bf16[20,1,128]{2,1,0:T(2,128)(2,1)S(1)}, bf16[20,1,128]{2,1,0:T(2,128)(2,1)S(1)}, u32[]{:S(2)}, u32[]{:S(2)}) collective-permute-start(bf16[20,1,128]{2,1,0:T(2,128)(2,1)S(1)} %slice.795), channel_id=1, source_target_pairs={{8,0},{16,8},{24,16},{32,24},{40,32},{48,40},{56,48},{64,56},{72,6... | collective-permute-start | bytes 15368 | tf_op jit(solution)/shard_map/ppermute | solution.py:13
  11.2 92.0 %copy-start.1 = (f32[2,20,8,128]{3,2,1,0:T(8,128)S(1)}, f32[2,20,8,128]{3,2,1,0:T(8,128)}, u32[]{:S(2)}) copy-start(f32[2,20,8,128]{3,2,1,0:T(8,128)} %param.12) | copy-start | bytes 491524
  13.2 8.8 %collective-permute-start.2 = (f32[2,20,1,128]{3,2,1,0:T(1,128)S(1)}, f32[2,20,1,128]{3,2,1,0:T(1,128)S(1)}, u32[]{:S(2)}, u32[]{:S(2)}) collective-permute-start(f32[2,20,1,128]{3,2,1,0:T(1,128)S(1)} %get-tuple-element.67), channel_id=1, source_target_pairs={{0,8},{8,16},{16,24},{24,32},{32,40},{40,48},{48,56},{56,64},{64,7... | collective-permute-start | bytes 61448 | tf_op jit(solution)/shard_map/ppermute | solution.py:24
  15.1 95.9 %copy-start.4 = (s32[1,1,256]{2,1,0:T(1,128)S(1)}, s32[1,1,256]{2,1,0:T(1,128)}, u32[]{:S(2)}) copy-start(s32[1,1,256]{2,1,0:T(1,128)} %param.19) | copy-start | bytes 3076
  15.1 95.9 %copy-start.3 = (bf16[4,20,8,128]{3,2,1,0:T(8,128)(2,1)S(1)}, bf16[4,20,8,128]{3,2,1,0:T(8,128)(2,1)}, u32[]{:S(2)}) copy-start(bf16[4,20,8,128]{3,2,1,0:T(8,128)(2,1)} %param.15) | copy-start | bytes 491524
  15.2 7.4 %collective-permute-start.3 = (f32[2,20,1,128]{3,2,1,0:T(1,128)S(1)}, f32[2,20,1,128]{3,2,1,0:T(1,128)S(1)}, u32[]{:S(2)}, u32[]{:S(2)}) collective-permute-start(f32[2,20,1,128]{3,2,1,0:T(1,128)S(1)} %get-tuple-element.68), channel_id=1, source_target_pairs={{8,0},{16,8},{24,16},{32,24},{40,32},{48,40},{56,48},{64,56},{72,6... | collective-permute-start | bytes 61448 | tf_op jit(solution)/shard_map/ppermute | solution.py:26
  22.7 12.1 %collective-permute-start.4 = (f32[2,20,10,1]{3,2,1,0:T(8,128)S(1)}, f32[2,20,10,1]{3,2,1,0:T(8,128)S(1)}, u32[]{:S(2)}, u32[]{:S(2)}) collective-permute-start(f32[2,20,10,1]{3,2,1,0:T(8,128)S(1)} %get-tuple-element.43), channel_id=1, source_target_pairs={{0,1},{1,2},{2,3},{3,4},{4,5},{5,6},{6,7},{8,9},{9,10},{10,11},{11... | collective-permute-start | bytes 4808 | tf_op jit(solution)/shard_map/ppermute | solution.py:24
  28.6 15.6 %collective-permute-start.5 = (f32[2,20,10,1]{3,2,1,0:T(8,128)S(1)}, f32[2,20,10,1]{3,2,1,0:T(8,128)S(1)}, u32[]{:S(2)}, u32[]{:S(2)}) collective-permute-start(f32[2,20,10,1]{3,2,1,0:T(8,128)S(1)} %get-tuple-element.44), channel_id=1, source_target_pairs={{1,0},{2,1},{3,2},{4,3},{5,4},{6,5},{7,6},{9,8},{10,9},{11,10},{12... | collective-permute-start | bytes 4808 | tf_op jit(solution)/shard_map/ppermute | solution.py:26
  45.6 7.7 %collective-permute-start.6 = (f32[2,20,1,128]{3,2,1,0:T(1,128)S(1)}, f32[2,20,1,128]{3,2,1,0:T(1,128)S(1)}, u32[]{:S(2)}, u32[]{:S(2)}) collective-permute-start(f32[2,20,1,128]{3,2,1,0:T(1,128)S(1)} %get-tuple-element.63), channel_id=1, source_target_pairs={{0,8},{8,16},{16,24},{24,32},{32,40},{40,48},{48,56},{56,64},{64,7... | collective-permute-start | bytes 61448 | tf_op jit(solution)/shard_map/ppermute | solution.py:24
  47.5 7.2 %collective-permute-start.7 = (f32[2,20,1,128]{3,2,1,0:T(1,128)S(1)}, f32[2,20,1,128]{3,2,1,0:T(1,128)S(1)}, u32[]{:S(2)}, u32[]{:S(2)}) collective-permute-start(f32[2,20,1,128]{3,2,1,0:T(1,128)S(1)} %get-tuple-element.64), channel_id=1, source_target_pairs={{8,0},{16,8},{24,16},{32,24},{40,32},{48,40},{56,48},{64,56},{72,6... | collective-permute-start | bytes 61448 | tf_op jit(solution)/shard_map/ppermute | solution.py:26
  54.9 9.2 %collective-permute-start.8 = (f32[2,20,10,1]{3,2,1,0:T(8,128)S(1)}, f32[2,20,10,1]{3,2,1,0:T(8,128)S(1)}, u32[]{:S(2)}, u32[]{:S(2)}) collective-permute-start(f32[2,20,10,1]{3,2,1,0:T(8,128)S(1)} %get-tuple-element.41), channel_id=1, source_target_pairs={{0,1},{1,2},{2,3},{3,4},{4,5},{5,6},{6,7},{8,9},{9,10},{10,11},{11... | collective-permute-start | bytes 4808 | tf_op jit(solution)/shard_map/ppermute | solution.py:24
  59.6 13.8 %collective-permute-start.9 = (f32[2,20,10,1]{3,2,1,0:T(8,128)S(1)}, f32[2,20,10,1]{3,2,1,0:T(8,128)S(1)}, u32[]{:S(2)}, u32[]{:S(2)}) collective-permute-start(f32[2,20,10,1]{3,2,1,0:T(8,128)S(1)} %get-tuple-element.42), channel_id=1, source_target_pairs={{1,0},{2,1},{3,2},{4,3},{5,4},{6,5},{7,6},{9,8},{10,9},{11,10},{12... | collective-permute-start | bytes 4808 | tf_op jit(solution)/shard_map/ppermute | solution.py:26
  73.8 7.7 %collective-permute-start.10 = (f32[2,20,1,128]{3,2,1,0:T(1,128)S(1)}, f32[2,20,1,128]{3,2,1,0:T(1,128)S(1)}, u32[]{:S(2)}, u32[]{:S(2)}) collective-permute-start(f32[2,20,1,128]{3,2,1,0:T(1,128)S(1)} %get-tuple-element.59), channel_id=1, source_target_pairs={{0,8},{8,16},{16,24},{24,32},{32,40},{40,48},{48,56},{56,64},{64,7... | collective-permute-start | bytes 61448 | tf_op jit(solution)/shard_map/ppermute | solution.py:24
  75.8 7.2 %collective-permute-start.11 = (f32[2,20,1,128]{3,2,1,0:T(1,128)S(1)}, f32[2,20,1,128]{3,2,1,0:T(1,128)S(1)}, u32[]{:S(2)}, u32[]{:S(2)}) collective-permute-start(f32[2,20,1,128]{3,2,1,0:T(1,128)S(1)} %get-tuple-element.60), channel_id=1, source_target_pairs={{8,0},{16,8},{24,16},{32,24},{40,32},{48,40},{56,48},{64,56},{72,6... | collective-permute-start | bytes 61448 | tf_op jit(solution)/shard_map/ppermute | solution.py:26
  83.2 10.2 %collective-permute-start.12 = (f32[2,20,10,1]{3,2,1,0:T(8,128)S(1)}, f32[2,20,10,1]{3,2,1,0:T(8,128)S(1)}, u32[]{:S(2)}, u32[]{:S(2)}) collective-permute-start(f32[2,20,10,1]{3,2,1,0:T(8,128)S(1)} %get-tuple-element.39), channel_id=1, source_target_pairs={{0,1},{1,2},{2,3},{3,4},{4,5},{5,6},{6,7},{8,9},{9,10},{10,11},{11... | collective-permute-start | bytes 4808 | tf_op jit(solution)/shard_map/ppermute | solution.py:24
  87.7 15.0 %collective-permute-start.13 = (f32[2,20,10,1]{3,2,1,0:T(8,128)S(1)}, f32[2,20,10,1]{3,2,1,0:T(8,128)S(1)}, u32[]{:S(2)}, u32[]{:S(2)}) collective-permute-start(f32[2,20,10,1]{3,2,1,0:T(8,128)S(1)} %get-tuple-element.40), channel_id=1, source_target_pairs={{1,0},{2,1},{3,2},{4,3},{5,4},{6,5},{7,6},{9,8},{10,9},{11,10},{12... | collective-permute-start | bytes 4808 | tf_op jit(solution)/shard_map/ppermute | solution.py:26
  103.4 7.8 %collective-permute-start.14 = (f32[2,20,1,128]{3,2,1,0:T(1,128)S(1)}, f32[2,20,1,128]{3,2,1,0:T(1,128)S(1)}, u32[]{:S(2)}, u32[]{:S(2)}) collective-permute-start(f32[2,20,1,128]{3,2,1,0:T(1,128)S(1)} %get-tuple-element.57), channel_id=1, source_target_pairs={{0,8},{8,16},{16,24},{24,32},{32,40},{40,48},{48,56},{56,64},{64,7... | collective-permute-start | bytes 61448 | tf_op jit(solution)/shard_map/ppermute | solution.py:24
  105.3 7.2 %collective-permute-start.15 = (f32[2,20,1,128]{3,2,1,0:T(1,128)S(1)}, f32[2,20,1,128]{3,2,1,0:T(1,128)S(1)}, u32[]{:S(2)}, u32[]{:S(2)}) collective-permute-start(f32[2,20,1,128]{3,2,1,0:T(1,128)S(1)} %get-tuple-element.58), channel_id=1, source_target_pairs={{8,0},{16,8},{24,16},{32,24},{40,32},{48,40},{56,48},{64,56},{72,6... | collective-permute-start | bytes 61448 | tf_op jit(solution)/shard_map/ppermute | solution.py:26
  112.7 9.1 %collective-permute-start.16 = (f32[2,20,10,1]{3,2,1,0:T(8,128)S(1)}, f32[2,20,10,1]{3,2,1,0:T(8,128)S(1)}, u32[]{:S(2)}, u32[]{:S(2)}) collective-permute-start(f32[2,20,10,1]{3,2,1,0:T(8,128)S(1)} %get-tuple-element.37), channel_id=1, source_target_pairs={{0,1},{1,2},{2,3},{3,4},{4,5},{5,6},{6,7},{8,9},{9,10},{10,11},{11... | collective-permute-start | bytes 4808 | tf_op jit(solution)/shard_map/ppermute | solution.py:24
  116.6 13.0 %collective-permute-start.17 = (f32[2,20,10,1]{3,2,1,0:T(8,128)S(1)}, f32[2,20,10,1]{3,2,1,0:T(8,128)S(1)}, u32[]{:S(2)}, u32[]{:S(2)}) collective-permute-start(f32[2,20,10,1]{3,2,1,0:T(8,128)S(1)} %get-tuple-element.38), channel_id=1, source_target_pairs={{1,0},{2,1},{3,2},{4,3},{5,4},{6,5},{7,6},{9,8},{10,9},{11,10},{12... | collective-permute-start | bytes 4808 | tf_op jit(solution)/shard_map/ppermute | solution.py:26
  130.1 7.7 %collective-permute-start.18 = (f32[2,20,1,128]{3,2,1,0:T(1,128)S(1)}, f32[2,20,1,128]{3,2,1,0:T(1,128)S(1)}, u32[]{:S(2)}, u32[]{:S(2)}) collective-permute-start(f32[2,20,1,128]{3,2,1,0:T(1,128)S(1)} %get-tuple-element.53), channel_id=1, source_target_pairs={{0,8},{8,16},{16,24},{24,32},{32,40},{40,48},{48,56},{56,64},{64,7... | collective-permute-start | bytes 61448 | tf_op jit(solution)/shard_map/ppermute | solution.py:24
  132.0 7.2 %collective-permute-start.19 = (f32[2,20,1,128]{3,2,1,0:T(1,128)S(1)}, f32[2,20,1,128]{3,2,1,0:T(1,128)S(1)}, u32[]{:S(2)}, u32[]{:S(2)}) collective-permute-start(f32[2,20,1,128]{3,2,1,0:T(1,128)S(1)} %get-tuple-element.54), channel_id=1, source_target_pairs={{8,0},{16,8},{24,16},{32,24},{40,32},{48,40},{56,48},{64,56},{72,6... | collective-permute-start | bytes 61448 | tf_op jit(solution)/shard_map/ppermute | solution.py:26
  139.5 7.7 %collective-permute-start.20 = (f32[2,20,10,1]{3,2,1,0:T(8,128)S(1)}, f32[2,20,10,1]{3,2,1,0:T(8,128)S(1)}, u32[]{:S(2)}, u32[]{:S(2)}) collective-permute-start(f32[2,20,10,1]{3,2,1,0:T(8,128)S(1)} %get-tuple-element.35), channel_id=1, source_target_pairs={{0,1},{1,2},{2,3},{3,4},{4,5},{5,6},{6,7},{8,9},{9,10},{10,11},{11... | collective-permute-start | bytes 4808 | tf_op jit(solution)/shard_map/ppermute | solution.py:24
  141.4 13.6 %collective-permute-start.21 = (f32[2,20,10,1]{3,2,1,0:T(8,128)S(1)}, f32[2,20,10,1]{3,2,1,0:T(8,128)S(1)}, u32[]{:S(2)}, u32[]{:S(2)}) collective-permute-start(f32[2,20,10,1]{3,2,1,0:T(8,128)S(1)} %get-tuple-element.36), channel_id=1, source_target_pairs={{1,0},{2,1},{3,2},{4,3},{5,4},{6,5},{7,6},{9,8},{10,9},{11,10},{12... | collective-permute-start | bytes 4808 | tf_op jit(solution)/shard_map/ppermute | solution.py:26
  142.7 48.7 %copy-start.5 = (s32[1,1,256]{2,1,0:T(1,128)S(1)}, s32[1,1,256]{2,1,0:T(1,128)}, u32[]{:S(2)}) copy-start(s32[1,1,256]{2,1,0:T(1,128)} %param.20) | copy-start | bytes 3076
  155.4 9.6 %collective-permute-start.22 = (f32[2,20,1,128]{3,2,1,0:T(1,128)S(1)}, f32[2,20,1,128]{3,2,1,0:T(1,128)S(1)}, u32[]{:S(2)}, u32[]{:S(2)}) collective-permute-start(f32[2,20,1,128]{3,2,1,0:T(1,128)S(1)} %get-tuple-element.49), channel_id=1, source_target_pairs={{0,8},{8,16},{16,24},{24,32},{32,40},{40,48},{48,56},{56,64},{64,7... | collective-permute-start | bytes 61448 | tf_op jit(solution)/shard_map/ppermute | solution.py:24
  157.3 7.7 %collective-permute-start.23 = (f32[2,20,1,128]{3,2,1,0:T(1,128)S(1)}, f32[2,20,1,128]{3,2,1,0:T(1,128)S(1)}, u32[]{:S(2)}, u32[]{:S(2)}) collective-permute-start(f32[2,20,1,128]{3,2,1,0:T(1,128)S(1)} %get-tuple-element.50), channel_id=1, source_target_pairs={{8,0},{16,8},{24,16},{32,24},{40,32},{48,40},{56,48},{64,56},{72,6... | collective-permute-start | bytes 61448 | tf_op jit(solution)/shard_map/ppermute | solution.py:26
  165.3 6.7 %collective-permute-start.24 = (f32[2,20,10,1]{3,2,1,0:T(8,128)S(1)}, f32[2,20,10,1]{3,2,1,0:T(8,128)S(1)}, u32[]{:S(2)}, u32[]{:S(2)}) collective-permute-start(f32[2,20,10,1]{3,2,1,0:T(8,128)S(1)} %get-tuple-element.33), channel_id=1, source_target_pairs={{0,1},{1,2},{2,3},{3,4},{4,5},{5,6},{6,7},{8,9},{9,10},{10,11},{11... | collective-permute-start | bytes 4808 | tf_op jit(solution)/shard_map/ppermute | solution.py:24
  166.8 13.0 %collective-permute-start.25 = (f32[2,20,10,1]{3,2,1,0:T(8,128)S(1)}, f32[2,20,10,1]{3,2,1,0:T(8,128)S(1)}, u32[]{:S(2)}, u32[]{:S(2)}) collective-permute-start(f32[2,20,10,1]{3,2,1,0:T(8,128)S(1)} %get-tuple-element.34), channel_id=1, source_target_pairs={{1,0},{2,1},{3,2},{4,3},{5,4},{6,5},{7,6},{9,8},{10,9},{11,10},{12... | collective-permute-start | bytes 4808 | tf_op jit(solution)/shard_map/ppermute | solution.py:26
  (1 other events, 48.7 us)
where the time goes:
time: 322 us; the launch traced here: 321 us
  blocking collectives  129 us (40%)
  waiting for transfers between devices  85.2 us (26%)
  starting transfers between devices  79.7 us (25%)
  local copies, waits for them, and re-layouts  12.6 us (4%)
  other arithmetic  11.9 us (4%)
    unnamed x1, blocking collectives  108 us
    ppermute x12, waiting for transfers between devices, extended(): lax.ppermute(head, axis, [((i + 1) % count, i) for i in range(ends)])  57.5 us
    ppermute x12, starting transfers between devices, extended(): lax.ppermute(head, axis, [((i + 1) % count, i) for i in range(ends)])  42.4 us
    ppermute x12, starting transfers between devices, extended(): lax.ppermute(tail, axis, [(i, (i + 1) % count) for i in range(ends)])  33.6 us
    ppermute x12, waiting for transfers between devices, extended(): lax.ppermute(tail, axis, [(i, (i + 1) % count) for i in range(ends)])  24.9 us
    psum x1, blocking collectives, per_device(): well_partials = lax.psum(owned, 'gy')  20.5 us
  transfers between devices with their start and end apart: 26, of which 18 were waited for; matrix products, arithmetic and copies ran while one was open for 1% of the time, Pallas kernels for 0%

commit v1 on v0

v1 whole, which is shorter than its diff:
```python
import functools

import jax
import jax.numpy as jnp
from jax import lax
from jax.experimental import pallas as pl
from jax.experimental.pallas import tpu as pltpu
from jax.sharding import PartitionSpec as P

MESH = pl.DeviceIdType.MESH
F32 = jnp.float32
BF16 = jnp.bfloat16
SWEEPS = 3
CHUNK = 4


def lanes(shape):
    return lax.broadcasted_iota(jnp.int32, shape, len(shape) - 1)


def rows_of(shape):
    return lax.broadcasted_iota(jnp.int32, shape, len(shape) - 2)


def halves(x):
    high = x.astype(BF16)
    return high, (x - high.astype(F32)).astype(BF16)


def onehot_dot(onehot, x):
    high, low = halves(x)
    return jnp.dot(onehot, high, preferred_element_type=F32) + jnp.dot(
        onehot, low, preferred_element_type=F32
    )


def kernel(
    n_gx, n_gy, nz,
    grad_late, grad_early, accum, mob_late, mob_early, trans_x, trans_y, trans_z,
    perf_cell, perf_well, productivity,
    early_out, wells_out,
    tx, txp, ty, typ, tz, k_late, k_early, inv_early, base_late, base_early, y_a, y_b,
    sx, rx, sy, ry, h_send, h_recv,
    cell_row, col_weight, pbuf, ra, sb, rb, a_send, a_recv, b_send, b_recv,
):
    i = lax.axis_index("gx")
    j = lax.axis_index("gy")
    group = 4
    a_count = group * n_gy
    per_dev = n_gx // a_count
    planes = n_gx // group
    plane, spot = i // group, i % group
    q = spot * n_gy + j
    left_right = (
        ((i + n_gx - 1) % n_gx, j),
        ((i + 1) % n_gx, j),
        (i, (j + n_gy - 1) % n_gy),
        (i, (j + 1) % n_gy),
    )

    def a_partner(d):
        t = (q + d) % a_count
        return t, (plane * group + t // n_gy, t % n_gy)

    barrier = pltpu.get_barrier_semaphore()
    greeted = 0
    for device in left_right:
        pl.semaphore_signal(barrier, inc=1, device_id=device, device_id_type=MESH)
        greeted += 1
    for d in range(1, a_count):
        pl.semaphore_signal(barrier, inc=1, device_id=a_partner(d)[1], device_id_type=MESH)
        greeted += 1
    source_q = i // per_dev
    for p in range(planes):
        pl.semaphore_signal(
            barrier, inc=1,
            device_id=(p * group + source_q // n_gy, source_q % n_gy), device_id_type=MESH,
        )
        greeted += 1

    sub = rows_of((CHUNK, 8, 128))
    lane = lanes((CHUNK, 8, 128))
    lane1 = lanes((8, 128))
    steps = nz // CHUNK

    tz[0] = jnp.zeros((8, 128), F32)
    tz[nz] = jnp.zeros((8, 128), F32)
    first_row = jnp.where(i == 0, 0, -1)
    first_col = jnp.where(j == 0, 0, -1)

    def load_trans(s, _):
        at = pl.ds(s * CHUNK, CHUNK)
        tx[at] = jnp.where(sub == first_row, 0.0, trans_x[at].astype(F32))
        ty[at] = jnp.where(lane == first_col, 0.0, trans_y[at].astype(F32))
        return 0

    lax.fori_loop(0, steps, load_trans, 0)
    for l in range(1, nz):
        tz[l] = trans_z[l].astype(F32)

    zero = jnp.zeros((8, 128), F32)
    for buf in (y_a, y_b):
        for c in range(2):
            buf[c, 0] = zero
            buf[c, nz + 1] = zero

    cells = jnp.transpose(jnp.broadcast_to(perf_cell[0], (128, 256)))
    wells = jnp.transpose(jnp.broadcast_to(perf_well[0], (128, 256)))
    prods = jnp.transpose(jnp.broadcast_to(productivity[0], (128, 256)))
    lane_p = lanes((256, 128))
    cell_line = cells // 128
    cell_row[:, 0:128] = jnp.where(cell_line == lane_p, 1.0, 0.0).astype(BF16)
    cell_row[:, 128:256] = jnp.where(cell_line == lane_p + 128, 1.0, 0.0).astype(BF16)
    col_weight[...] = jnp.where(cells % 128 == lane_p, prods, 0.0)

    pl.semaphore_wait(barrier, greeted)

    started = []

    def exchange(r, row_first, row_last, packs):
        for c in range(2):
            for l in range(nz):
                sx[r, 0, c * nz + l] = row_first(c, l)
                sx[r, 1, c * nz + l] = row_last(c, l)
            sy[r, c] = packs(c)
        copies = []
        for k, device in enumerate(left_right):
            if k < 2:
                src, dst = sx.at[r, k], rx.at[r, 1 - k]
            else:
                src, dst = sy.at[r], ry.at[r, 3 - k]
            copy = pltpu.make_async_remote_copy(
                src_ref=src, dst_ref=dst, send_sem=h_send.at[r, k], recv_sem=h_recv.at[r, k],
                device_id=device, device_id_type=MESH,
            )
            copy.start()
            copies.append(copy)
        for copy in copies:
            copy.wait_recv()
        started.extend(copies)

    def pack(plane_of):
        out = zero
        for l in range(nz):
            rolled = pltpu.roll(plane_of(l), 1 + 2 * l, 1)
            out = jnp.where(lane1 // 2 == l, rolled, out)
        return out

    def sides(r, c):
        return jnp.where(lane1 % 2 == 0, ry[r, 0, c], ry[r, 1, c])

    def unpack(packed, s):
        return jnp.stack(
            [pltpu.roll(packed, 127 - 2 * (s * CHUNK + t), 1) for t in range(CHUNK)]
        )

    exchange(
        0,
        lambda c, l: tx[l, 0:1], lambda c, l: tx[l, 0:1],
        lambda c: pack(lambda l: ty[l]),
    )
    ty_side = sides(0, 0)

    def far_faces(s, _):
        at = pl.ds(s * CHUNK, CHUNK)
        above = rx[0, 1, at]
        txp[at] = jnp.where(sub == 7, above, pltpu.roll(tx[at], 7, 1))
        ends = unpack(ty_side, s)
        typ[at] = pltpu.roll(jnp.where(lane == 0, ends, ty[at]), 127, 2)
        return 0

    lax.fori_loop(0, steps, far_faces, 0)

    def setup(mob, k_out, inv_out, y_out, base_out, source):
        def body(s, _):
            at = pl.ds(s * CHUNK, CHUNK)
            faces = tx[at] + txp[at] + ty[at] + typ[at] + tz[at] + tz[pl.ds(s * CHUNK + 1, CHUNK)]
            b = [mob[k, at].astype(F32) for k in range(4)]
            d = [accum[k, at].astype(F32) + faces * b[k] for k in range(4)]
            scale = 1.0 / (d[0] * d[3] - d[1] * d[2])
            inv = [d[3] * scale, -d[1] * scale, -d[2] * scale, d[0] * scale]
            k_out[0, at] = inv[0] * b[0] + inv[2] * b[1]
            k_out[1, at] = inv[0] * b[2] + inv[2] * b[3]
            k_out[2, at] = inv[1] * b[0] + inv[3] * b[1]
            k_out[3, at] = inv[1] * b[2] + inv[3] * b[3]
            if inv_out is not None:
                for k in range(4):
                    inv_out[k, at] = inv[k]
            if source is not None:
                v = [source[c, at] for c in range(2)]
                at1 = pl.ds(s * CHUNK + 1, CHUNK)
                y0 = inv[0] * v[0] + inv[2] * v[1]
                y1 = inv[1] * v[0] + inv[3] * v[1]
                base_out[0, at] = y0
                base_out[1, at] = y1
                y_out[0, at1] = y0
                y_out[1, at1] = y1
            return 0

        lax.fori_loop(0, steps, body, 0)

    setup(mob_late, k_late, None, y_a, base_late, grad_late)
    setup(mob_early, k_early, inv_early, None, None, None)

    def sweep(r, y, k_mat, base, y_out, shift_out):
        exchange(
            r,
            lambda c, l: y[c, l + 1, 0:1], lambda c, l: y[c, l + 1, 7:8],
            lambda c: pack(lambda l: y[c, l + 1]),
        )
        side = [sides(r, c) for c in range(2)]

        def body(s, _):
            at = pl.ds(s * CHUNK, CHUNK)
            at1 = pl.ds(s * CHUNK + 1, CHUNK)
            at2 = pl.ds(s * CHUNK + 2, CHUNK)
            flow = []
            for c in range(2):
                mid = y[c, at1]
                below = rx[r, 0, pl.ds(c * nz + s * CHUNK, CHUNK)]
                above = rx[r, 1, pl.ds(c * nz + s * CHUNK, CHUNK)]
                ends = unpack(side[c], s)
                x_low = jnp.where(sub == 0, below, pltpu.roll(mid, 1, 1))
                x_high = jnp.where(sub == 7, above, pltpu.roll(mid, 7, 1))
                y_low = pltpu.roll(jnp.where(lane == 127, ends, mid), 1, 2)
                y_high = pltpu.roll(jnp.where(lane == 0, ends, mid), 127, 2)
                flow.append(
                    tx[at] * x_low + txp[at] * x_high + ty[at] * y_low + typ[at] * y_high
                    + tz[at] * y[c, at] + tz[at1] * y[c, at2]
                )
            for c in range(2):
                y_out[c, pl.ds(s * CHUNK + shift_out, CHUNK)] = (
                    base[c, at] + k_mat[2 * c, at] * flow[0] + k_mat[2 * c + 1, at] * flow[1]
                )
            return 0

        lax.fori_loop(0, steps, body, 0)

    sweep(1, y_a, k_late, base_late, y_b, 1)
    sweep(2, y_b, k_late, base_late, y_a, 1)
    sweep(3, y_a, k_late, base_late, y_b, 1)

    pad = jnp.zeros((256 - 8 * nz, 128), F32)

    def picked(field):
        lines = jnp.concatenate([field.reshape(8 * nz, 128), pad], 0)
        terms = onehot_dot(cell_row[...], lines) * col_weight[...]
        return jnp.sum(terms, axis=1, keepdims=True)

    own_lane = lane_p - wells % 8
    spread = jnp.zeros((256, 128), F32)
    for c in range(2):
        spread = jnp.where(own_lane == 8 * (c + 2), picked(y_b[c, pl.ds(1, nz)]), spread)

    def start_early(s, _):
        at = pl.ds(s * CHUNK, CHUNK)
        at1 = pl.ds(s * CHUNK + 1, CHUNK)
        late = [y_b[c, at1] for c in range(2)]
        a = [accum[k, at].astype(F32) for k in range(4)]
        v0 = grad_early[0, at] + a[0] * late[0] + a[2] * late[1]
        v1 = grad_early[1, at] + a[1] * late[0] + a[3] * late[1]
        y0 = inv_early[0, at] * v0 + inv_early[2, at] * v1
        y1 = inv_early[1, at] * v0 + inv_early[3, at] * v1
        base_early[0, at] = y0
        base_early[1, at] = y1
        y_a[0, at1] = y0
        y_a[1, at1] = y1
        return 0

    lax.fori_loop(0, steps, start_early, 0)
    sweep(4, y_a, k_early, base_early, y_b, 1)
    sweep(5, y_b, k_early, base_early, y_a, 1)
    sweep(6, y_a, k_early, base_early, early_out, 0)

    for c in range(2):
        spread = jnp.where(own_lane == 8 * c, picked(early_out[c]), spread)
    owner = jnp.where(
        rows_of((n_gx, 256)) == jnp.broadcast_to(perf_well[0] // 8, (n_gx, 256)), 1.0, 0.0
    ).astype(BF16)
    partial = onehot_dot(owner, spread)
    for o in range(n_gx):
        pbuf[o] = partial[o : o + 1]

    for d in range(1, a_count):
        t, device = a_partner(d)
        copy = pltpu.make_async_remote_copy(
            src_ref=pbuf.at[pl.ds(t * per_dev, per_dev)], dst_ref=ra.at[pl.ds(d * per_dev, per_dev)],
            send_sem=a_send.at[d], recv_sem=a_recv, device_id=device, device_id_type=MESH,
        )
        copy.start()
        started.append(copy)
    landed = ra.at[pl.ds(per_dev, n_gx - per_dev)]
    pltpu.make_async_copy(landed, landed, a_recv).wait()
    for r in range(per_dev):
        total = pbuf[q * per_dev + r]
        for d in range(1, a_count):
            total = total + ra[d * per_dev + r]
        sb[r] = total

    def b_copy(r, dest_j):
        dest_i = q * per_dev + r
        own = jnp.logical_and(dest_i == i, j == dest_j)
        return own, pltpu.make_async_remote_copy(
            src_ref=sb.at[r], dst_ref=rb.at[plane], send_sem=b_send.at[r * n_gy + dest_j], recv_sem=b_recv,
            device_id=(dest_i, dest_j), device_id_type=MESH,
        )

    for r in range(per_dev):
        for dest_j in range(n_gy):
            own, copy = b_copy(r, dest_j)
            pl.when(jnp.logical_not(own))(copy.start)
            pl.when(own)(pltpu.make_async_copy(sb.at[r], rb.at[plane], b_recv).start)
    pltpu.make_async_copy(rb, rb, b_recv).wait()
    total = rb[0]
    for p in range(1, planes):
        total = total + rb[p]
    total = jnp.broadcast_to(total, (8, 128))
    out = total
    for k in range(1, 4):
        out = jnp.where(rows_of((8, 128)) == k, pltpu.roll(total, 128 - 8 * k, 1), out)
    wells_out[...] = out[0:4, 0:8]

    for copy in started:
        copy.wait_send()
    for r in range(per_dev):
        for dest_j in range(n_gy):
            own, copy = b_copy(r, dest_j)
            pl.when(jnp.logical_not(own))(copy.wait_send)


def per_device(n_gx, n_gy, *args):
    nz = args[5].shape[0]
    rounds = 2 * SWEEPS + 1
    a_count = 4 * n_gy
    per_dev = n_gx // a_count
    planes = n_gx // 4
    field = pltpu.VMEM((nz, 8, 128), F32)
    field2 = pltpu.VMEM((2, nz, 8, 128), F32)
    field4 = pltpu.VMEM((4, nz, 8, 128), F32)
    padded = pltpu.VMEM((2, nz + 2, 8, 128), F32)
    dma = pltpu.SemaphoreType.DMA
    vmem = pl.BlockSpec(memory_space=pltpu.VMEM)
    return pl.pallas_call(
        functools.partial(kernel, n_gx, n_gy, nz),
        out_shape=(
            jax.ShapeDtypeStruct((2, nz, 8, 128), F32),
            jax.ShapeDtypeStruct((4, 8), F32),
        ),
        in_specs=[vmem] * 11,
        out_specs=(vmem, vmem),
        scratch_shapes=[
            field, field, field, field, pltpu.VMEM((nz + 1, 8, 128), F32),
            field4, field4, field4, field2, field2, padded, padded,
            pltpu.VMEM((rounds, 2, 2 * nz, 1, 128), F32),
            pltpu.VMEM((rounds, 2, 2 * nz, 1, 128), F32),
            pltpu.VMEM((rounds, 2, 8, 128), F32),
            pltpu.VMEM((rounds, 2, 2, 8, 128), F32),
            dma((rounds, 4)), dma((rounds, 4)),
            pltpu.VMEM((256, 256), BF16), pltpu.VMEM((256, 128), F32),
            pltpu.VMEM((n_gx, 1, 128), F32), pltpu.VMEM((n_gx, 1, 128), F32),
            pltpu.VMEM((per_dev, 1, 128), F32), pltpu.VMEM((planes, 1, 128), F32),
            dma((a_count,)), dma, dma((per_dev * n_gy,)), dma,
        ],
        compiler_params=pltpu.CompilerParams(
            collective_id=0, has_side_effects=True, vmem_limit_bytes=40 * 1024 * 1024
        ),
    )(*args)


def solution(mesh):
    n_gx, n_gy = mesh.shape["gx"], mesh.shape["gy"]
    cells = P(None, None, "gx", "gy")
    faces = P(None, "gx", "gy")
    perfs = P("gx", "gy", None)
    return jax.shard_map(
        functools.partial(per_device, n_gx, n_gy),
        mesh=mesh,
        in_specs=(cells,) * 5 + (faces,) * 3 + (perfs,) * 3,
        out_specs=(cells, P(None, "gx")),
        check_vma=False,
    )
```

time: 322 us -> 81.6 us (0.25)
  the two profiles are of different devices: /device:TPU:128 before, /device:TPU:1 now
where the time goes in v1:
time: 81.6 us; the launch traced here: 81.2 us
  Pallas kernels  70.3 us (86%)
  local copies, waits for them, and re-layouts  10.2 us (12%)
    pallas_call x1, Pallas kernels, per_device(): pl.pallas_call(functools.partial(kernel, n_gx, n_gy, nz), out_shape=(jax....  70.3 us
    unnamed x24, local copies, waits for them, and re-layouts  10.2 us

profile of v1, /device:TPU:1, one launch (start us, length us, event | category | flops | bytes accessed | tf_op | source)
XLA Modules:
  0.0 81.2 jit_solution(9167021672086450976)
XLA Ops:
  0.6 0.0 copy-start
  0.6 0.9 %copy-done = f32[2,20,8,128]{3,2,1,0:T(8,128)S(1)} copy-done((f32[2,20,8,128]{3,2,1,0:T(8,128)S(1)}, f32[2,20,8,128]{3,2,1,0:T(8,128)}, u32[]{:S(2)}) %copy-start) | copy-done | bytes 163864
  1.6 0.0 copy-start.1
  1.6 0.9 %copy-done.1 = f32[2,20,8,128]{3,2,1,0:T(8,128)S(1)} copy-done((f32[2,20,8,128]{3,2,1,0:T(8,128)S(1)}, f32[2,20,8,128]{3,2,1,0:T(8,128)}, u32[]{:S(2)}) %copy-start.1) | copy-done | bytes 163864
  2.5 0.0 copy-start.2
  2.5 0.9 %copy-done.2 = bf16[4,20,8,128]{3,2,1,0:T(8,128)(2,1)S(1)} copy-done((bf16[4,20,8,128]{3,2,1,0:T(8,128)(2,1)S(1)}, bf16[4,20,8,128]{3,2,1,0:T(8,128)(2,1)}, u32[]{:S(2)}) %copy-start.2) | copy-done | bytes 163864
  3.4 0.0 copy-start.3
  3.4 0.9 %copy-done.3 = bf16[4,20,8,128]{3,2,1,0:T(8,128)(2,1)S(1)} copy-done((bf16[4,20,8,128]{3,2,1,0:T(8,128)(2,1)S(1)}, bf16[4,20,8,128]{3,2,1,0:T(8,128)(2,1)}, u32[]{:S(2)}) %copy-start.3) | copy-done | bytes 163864
  4.3 0.0 copy-start.4
  4.3 0.9 %copy-done.4 = bf16[4,20,8,128]{3,2,1,0:T(8,128)(2,1)S(1)} copy-done((bf16[4,20,8,128]{3,2,1,0:T(8,128)(2,1)S(1)}, bf16[4,20,8,128]{3,2,1,0:T(8,128)(2,1)}, u32[]{:S(2)}) %copy-start.4) | copy-done | bytes 163864
  5.2 0.0 copy-start.5
  5.2 0.8 copy-done.5
  6.0 0.0 copy-start.6
  6.0 0.8 copy-done.6
  6.8 0.0 copy-start.7
  6.8 0.8 copy-done.7
  7.6 0.0 copy-start.8
  7.6 0.7 copy-done.8
  8.2 0.0 copy-start.9
  8.2 0.7 copy-done.9
  8.9 0.0 copy-start.10
  8.9 0.7 copy-done.10
  9.6 70.3 %shard_map.122 = (f32[2,20,8,128]{3,2,1,0:T(8,128)S(1)}, f32[4,8]{1,0:T(4,128)S(1)}) custom-call(f32[2,20,8,128]{3,2,1,0:T(8,128)S(1)} %copy-done, f32[2,20,8,128]{3,2,1,0:T(8,128)S(1)} %copy-done.1, bf16[4,20,8,128]{3,2,1,0:T(8,128)(2,1)S(1)} %copy-done.2, bf16[4,20,8,128]{3,2,1,0:T(8,128)(2,1)S(1)} %copy-done.3, bf16[4,20,8,128]{3,2,1,0:T(8,128)(2,1)S(1)} %copy-done.4, ...), custom_call_target="tpu_custom_call" | custom-call | tf_op jit(solution)/shard_map/pallas_call | solution.py:343
  79.9 0.7 copy.15
  80.6 0.6 copy.16
Async XLA Ops:
  0.6 0.9 %copy-start = (f32[2,20,8,128]{3,2,1,0:T(8,128)S(1)}, f32[2,20,8,128]{3,2,1,0:T(8,128)}, u32[]{:S(2)}) copy-start(f32[2,20,8,128]{3,2,1,0:T(8,128)} %grad_late.1) | copy-start | bytes 491524
  1.6 0.9 %copy-start.1 = (f32[2,20,8,128]{3,2,1,0:T(8,128)S(1)}, f32[2,20,8,128]{3,2,1,0:T(8,128)}, u32[]{:S(2)}) copy-start(f32[2,20,8,128]{3,2,1,0:T(8,128)} %grad_early.1) | copy-start | bytes 491524
  2.5 0.9 %copy-start.2 = (bf16[4,20,8,128]{3,2,1,0:T(8,128)(2,1)S(1)}, bf16[4,20,8,128]{3,2,1,0:T(8,128)(2,1)}, u32[]{:S(2)}) copy-start(bf16[4,20,8,128]{3,2,1,0:T(8,128)(2,1)} %accum.1) | copy-start | bytes 491524
  3.4 0.9 %copy-start.3 = (bf16[4,20,8,128]{3,2,1,0:T(8,128)(2,1)S(1)}, bf16[4,20,8,128]{3,2,1,0:T(8,128)(2,1)}, u32[]{:S(2)}) copy-start(bf16[4,20,8,128]{3,2,1,0:T(8,128)(2,1)} %mob_late.1) | copy-start | bytes 491524
  4.3 0.9 %copy-start.4 = (bf16[4,20,8,128]{3,2,1,0:T(8,128)(2,1)S(1)}, bf16[4,20,8,128]{3,2,1,0:T(8,128)(2,1)}, u32[]{:S(2)}) copy-start(bf16[4,20,8,128]{3,2,1,0:T(8,128)(2,1)} %mob_early.1) | copy-start | bytes 491524
  5.2 0.8 copy-start.5
  6.0 0.8 copy-start.6
  6.8 0.8 copy-start.7
  7.6 0.7 copy-start.8
  8.2 0.7 copy-start.9
  8.9 0.7 copy-start.10

commit v2 on v1

--- a/solution.py
+++ b/solution.py
@@ -36,13 +36,20 @@
 
 def kernel(
     n_gx, n_gy, nz,
-    grad_late, grad_early, accum, mob_late, mob_early, trans_x, trans_y, trans_z,
-    perf_cell, perf_well, productivity,
-    early_out, wells_out,
-    tx, txp, ty, typ, tz, k_late, k_early, inv_early, base_late, base_early, y_a, y_b,
-    sx, rx, sy, ry, h_send, h_recv,
-    cell_row, col_weight, pbuf, ra, sb, rb, a_send, a_recv, b_send, b_recv,
+    *refs,
 ):
+    inputs, (early_out, wells_out) = refs[:11], refs[11:13]
+    held, refs = refs[13:24], refs[24:]
+    (
+        in_sem,
+        tx, txp, ty, typ, tz, k_late, k_early, inv_early, base_late, base_early, y_a, y_b,
+        sx, rx, sy, ry, h_send, h_recv,
+        cell_row, col_weight, pbuf, ra, sb, rb, a_send, a_recv, b_send, b_recv, hello,
+    ) = refs
+    (
+        grad_late, grad_early, accum, mob_late, mob_early, trans_x, trans_y, trans_z,
+        perf_cell, perf_well, productivity,
+    ) = held
     i = lax.axis_index("gx")
     j = lax.axis_index("gy")
     group = 4
@@ -62,21 +69,24 @@
         t = (q + d) % a_count
         return t, (plane * group + t // n_gy, t % n_gy)
 
+    loads = [
+        pltpu.make_async_copy(inputs[k], held[k], in_sem.at[k])
+        for k in (5, 6, 7, 3, 2, 0, 4, 1, 8, 9, 10)
+    ]
+    for load in loads:
+        load.start()
+
+    def mate(distance):
+        return ((i + group * distance + n_gx) % n_gx, j)
+
+    near = [mate(d) for d in (-3, -2, -1, 1, 2, 3)]
+    far = [mate(d) for d in (-5, 5)]
     barrier = pltpu.get_barrier_semaphore()
-    greeted = 0
-    for device in left_right:
+    greeted = [*left_right[:2], *near] + [a_partner(d)[1] for d in range(1, a_count)]
+    for device in greeted:
         pl.semaphore_signal(barrier, inc=1, device_id=device, device_id_type=MESH)
-        greeted += 1
-    for d in range(1, a_count):
-        pl.semaphore_signal(barrier, inc=1, device_id=a_partner(d)[1], device_id_type=MESH)
-        greeted += 1
-    source_q = i // per_dev
-    for p in range(planes):
-        pl.semaphore_signal(
-            barrier, inc=1,
-            device_id=(p * group + source_q // n_gy, source_q % n_gy), device_id_type=MESH,
-        )
-        greeted += 1
+    for load in loads:
+        load.wait()
 
     sub = rows_of((CHUNK, 8, 128))
     lane = lanes((CHUNK, 8, 128))
@@ -113,7 +123,9 @@
     cell_row[:, 128:256] = jnp.where(cell_line == lane_p + 128, 1.0, 0.0).astype(BF16)
     col_weight[...] = jnp.where(cells % 128 == lane_p, prods, 0.0)
 
-    pl.semaphore_wait(barrier, greeted)
+    pl.semaphore_wait(barrier, len(greeted))
+    for device in near:
+        pl.semaphore_signal(hello.at[0], inc=1, device_id=device, device_id_type=MESH)
 
     started = []
 
@@ -236,6 +248,9 @@
 
         lax.fori_loop(0, steps, body, 0)
 
+    pl.semaphore_wait(hello.at[0], len(near))
+    for device in far:
+        pl.semaphore_signal(hello.at[1], inc=1, device_id=device, device_id_type=MESH)
     sweep(1, y_a, k_late, base_late, y_b, 1)
     sweep(2, y_b, k_late, base_late, y_a, 1)
     sweep(3, y_a, k_late, base_late, y_b, 1)
@@ -297,6 +312,7 @@
             total = total + ra[d * per_dev + r]
         sb[r] = total
 
+    pl.semaphore_wait(hello.at[1], len(far))
     def b_copy(r, dest_j):
         dest_i = q * per_dev + r
         own = jnp.logical_and(dest_i == i, j == dest_j)
@@ -346,9 +362,10 @@
             jax.ShapeDtypeStruct((2, nz, 8, 128), F32),
             jax.ShapeDtypeStruct((4, 8), F32),
         ),
-        in_specs=[vmem] * 11,
+        in_specs=[pl.BlockSpec(memory_space=pltpu.HBM)] * 11,
         out_specs=(vmem, vmem),
-        scratch_shapes=[
+        scratch_shapes=[pltpu.VMEM(a.shape, a.dtype) for a in args] + [
+            dma((11,)),
             field, field, field, field, pltpu.VMEM((nz + 1, 8, 128), F32),
             field4, field4, field4, field2, field2, padded, padded,
             pltpu.VMEM((rounds, 2, 2 * nz, 1, 128), F32),
@@ -360,9 +377,10 @@
             pltpu.VMEM((n_gx, 1, 128), F32), pltpu.VMEM((n_gx, 1, 128), F32),
             pltpu.VMEM((per_dev, 1, 128), F32), pltpu.VMEM((planes, 1, 128), F32),
             dma((a_count,)), dma, dma((per_dev * n_gy,)), dma,
+            pltpu.SemaphoreType.REGULAR((2,)),
         ],
         compiler_params=pltpu.CompilerParams(
-            collective_id=0, has_side_effects=True, vmem_limit_bytes=40 * 1024 * 1024
+            collective_id=0, has_side_effects=True, vmem_limit_bytes=60 * 1024 * 1024
         ),
     )(*args)
 

time: 81.6 us -> 72.9 us (0.89)
  local copies, waits for them, and re-layouts: 10.2 us -> 2.18 us
    unnamed x24 -> x4, local copies, waits for them, and re-layouts: 10.2 us -> 2.18 us
where the time goes in v2:
time: 72.9 us; the launch traced here: 72.8 us
  Pallas kernels  69.9 us (96%)
  local copies, waits for them, and re-layouts  2.18 us (3%)
    pallas_call x1, Pallas kernels, per_device(): pl.pallas_call(functools.partial(kernel, n_gx, n_gy, nz), out_shape=(jax....  69.9 us
    unnamed x4, local copies, waits for them, and re-layouts  2.18 us

profile of v2, /device:TPU:1, one launch (start us, length us, event | category | flops | bytes accessed | tf_op | source)
XLA Modules:
  0.0 72.8 jit_solution(15417209739727953128)
XLA Ops:
  0.6 69.9 %shard_map.122 = (f32[2,20,8,128]{3,2,1,0:T(8,128)}, f32[4,8]{1,0:T(4,128)}) custom-call(f32[2,20,8,128]{3,2,1,0:T(8,128)} %refs_0_.1, f32[2,20,8,128]{3,2,1,0:T(8,128)} %refs_1_.1, bf16[4,20,8,128]{3,2,1,0:T(8,128)(2,1)} %refs_2_.1, bf16[4,20,8,128]{3,2,1,0:T(8,128)(2,1)} %refs_3_.1, bf16[4,20,8,128]{3,2,1,0:T(8,128)(2,1)} %refs_4_.1, ...), custom_call_target="tpu_custom_call" | custom-call | tf_op jit(solution)/shard_map/pallas_call | solution.py:359
  70.6 0.0 copy-start
  70.6 1.6 %copy.15 = f32[2,20,8,128]{3,2,1,0:T(8,128)} copy(f32[2,20,8,128]{3,2,1,0:T(8,128)} %get-tuple-element.4) | data formatting | bytes 327680
  72.2 0.0 copy-done
  72.2 0.6 copy.16
Async XLA Ops:
  70.6 1.6 %copy-start = (f32[4,8]{1,0:T(4,128)S(1)}, f32[4,8]{1,0:T(4,128)}, u32[]{:S(2)}) copy-start(f32[4,8]{1,0:T(4,128)} %get-tuple-element.5) | copy-start | bytes 388

commit v3 on v2

v3 whole, which is shorter than its diff:
```python
import functools

import jax
import jax.numpy as jnp
from jax import lax
from jax.experimental import pallas as pl
from jax.experimental.pallas import tpu as pltpu
from jax.sharding import PartitionSpec as P

MESH = pl.DeviceIdType.MESH
F32 = jnp.float32
BF16 = jnp.bfloat16
PACK = 4
CHUNK = 2
WIDE = 6


def iota(shape, dim):
    return lax.broadcasted_iota(jnp.int32, shape, dim)


def onehot_dot(onehot, x):
    high = x.astype(BF16)
    low = (x - high.astype(F32)).astype(BF16)
    return jnp.dot(onehot, high, preferred_element_type=F32) + jnp.dot(
        onehot, low, preferred_element_type=F32
    )


def sub_of(x):
    return iota(x.shape, x.ndim - 2)


def row_shift(a, b, amount):
    ra, rb = pltpu.roll(a, amount, a.ndim - 2), pltpu.roll(b, amount, b.ndim - 2)
    edge = sub_of(a) == (0 if amount == 1 else 7)
    return jnp.where(edge, rb, ra), jnp.where(edge, ra, rb)


def pack_rows(x):
    x = x.reshape(x.shape[0] // 2, 2, 8, 128)
    even, odd = x[:, 0], pltpu.roll(x[:, 1], 4, 1)
    first = sub_of(even) < 4
    return jnp.where(first, odd, even), jnp.where(first, even, odd)


def unpack_rows(low, high):
    first = sub_of(low) < 4
    even = jnp.where(first, high, low)
    odd = pltpu.roll(jnp.where(first, low, high), 4, 1)
    return jnp.stack([even, odd], 1).reshape(2 * low.shape[0], 8, 128)


def block_system(accum, mob, faces, live=None):
    d = [accum[k] + faces * mob[k] for k in range(4)]
    det = d[0] * d[3] - d[1] * d[2]
    if live is not None:
        det = jnp.where(live, det, 1.0)
    scale = 1.0 / det
    inv = [d[3] * scale, -d[1] * scale, -d[2] * scale, d[0] * scale]
    b = mob
    mat = [
        inv[0] * b[0] + inv[2] * b[1],
        inv[0] * b[2] + inv[2] * b[3],
        inv[1] * b[0] + inv[3] * b[1],
        inv[1] * b[2] + inv[3] * b[3],
    ]
    return inv, mat


def transpose_apply(m, v):
    return [m[0] * v[0] + m[2] * v[1], m[1] * v[0] + m[3] * v[1]]


def kernel(n_gx, n_gy, nz, *refs):
    inputs, (early_out, wells_out), held = refs[:11], refs[11:13], refs[13:24]
    (
        in_sem, tx, txp, ty, typ, tz, k_late, k_early, inv_early, base_late, base_early, y_a, y_b,
        rim_faces, rim_k_late, rim_k_early, rim_late, rim_early, rim_a, rim_b,
        xs_bf, xs_f, xs_me, xs_e, xr_bf, xr_f, xr_me, xr_e, x_send, x_recv,
        ys_bf, ys_f, ys_me, ys_e, yr_bf, yr_f, yr_me, yr_e, y_send, y_recv,
        cell_row, col_weight, pbuf, ra, sb, rb, a_send, a_recv, b_send, b_recv, hello,
    ) = refs[24:]
    (
        grad_late, grad_early, accum, mob_late, mob_early, trans_x, trans_y, trans_z,
        perf_cell, perf_well, productivity,
    ) = held
    i = lax.axis_index("gx")
    j = lax.axis_index("gy")
    group = 4
    a_count = group * n_gy
    per_dev = n_gx // a_count
    planes = n_gx // group
    plane, spot = i // group, i % group
    q = spot * n_gy + j
    lower, upper = (i + n_gx - 1) % n_gx, (i + 1) % n_gx
    left, right = (j + n_gy - 1) % n_gy, (j + 1) % n_gy
    row_peers = ((upper, j), (lower, j))
    col_peers = ((i, right), (i, left), (lower, right), (lower, left), (upper, right), (upper, left))

    def a_partner(d):
        t = (q + d) % a_count
        return t, (plane * group + t // n_gy, t % n_gy)

    loads = [
        pltpu.make_async_copy(inputs[k], held[k], in_sem.at[k])
        for k in (5, 6, 7, 3, 2, 0, 4, 1, 8, 9, 10)
    ]
    for load in loads:
        load.start()

    def mate(distance):
        return ((i + group * distance + n_gx) % n_gx, j)

    near = [mate(d) for d in (-3, -2, -1, 1, 2, 3)]
    far = [mate(d) for d in (-5, 5)]
    barrier = pltpu.get_barrier_semaphore()
    greeted = [*row_peers, *col_peers, *near] + [a_partner(d)[1] for d in range(1, a_count)]
    for device in greeted:
        pl.semaphore_signal(barrier, inc=1, device_id=device, device_id_type=MESH)
    for load in loads:
        load.wait()

    zero = jnp.zeros((8, 128), F32)
    lane1 = iota((8, 128), 1)
    sub1 = iota((8, 128), 0)
    layer_of = lane1 // WIDE
    col_of = lane1 % WIDE
    live = lane1 < WIDE * nz
    packs = nz // PACK
    steps = nz // CHUNK
    first_row = jnp.where(i == 0, 0, -1)
    first_col = jnp.where(j == 0, 0, -1)

    def pack_cols(old, x, layer, extra=3):
        return jnp.where(layer_of == layer, pltpu.roll(x, extra + WIDE * layer, 1), old)

    def put_rows(x, s, send, k):
        last, first = pack_rows(x)
        if send.dtype == BF16:
            send[0, k, s] = last.reshape(4 * PACK, 128).astype(BF16)
            send[1, k, s] = first.reshape(4 * PACK, 128).astype(BF16)
        else:
            send[0, k, pl.ds(2 * s, 2)] = last
            send[1, k, pl.ds(2 * s, 2)] = first

    def first_out(s, cols):
        at = pl.ds(s * PACK, PACK)
        row, col = iota((PACK, 8, 128), 1), iota((PACK, 8, 128), 2)
        fx = jnp.where(row == first_row, 0.0, trans_x[at].astype(F32))
        fy = jnp.where(col == first_col, 0.0, trans_y[at].astype(F32))
        fz = jnp.where(iota((PACK, 8, 128), 0) + s * PACK == 0, 0.0, trans_z[at].astype(F32))
        tx[0, at] = fx
        ty[0, at] = fy
        tz[0, at] = fz
        fields = [mob_late[k, at].astype(F32) for k in range(4)]
        fields += [accum[k, at].astype(F32) for k in range(4)] + [fx, fy, fz]
        for k, x in enumerate(fields):
            put_rows(x, s, xs_bf, k)
        grads = [grad_late[c, at] for c in range(2)]
        for k, x in enumerate(grads):
            put_rows(x, s, xs_f, k)
        early = [mob_early[k, at].astype(F32) for k in range(4)]
        for k, x in enumerate(early):
            put_rows(x, s, xs_me, k)
        cols = list(cols)
        for t in range(PACK):
            layer = s * PACK + t
            for k, x in enumerate(fields + [fy] + grads + early):
                cols[k] = pack_cols(cols[k], x[t], layer, 2 if k == 11 else 3)
        return tuple(cols)

    cols = lax.fori_loop(0, packs, first_out, (zero,) * 18)
    for k in range(6):
        ys_bf[k] = jnp.concatenate([cols[2 * k], cols[2 * k + 1]], 0).astype(BF16)
    for k in range(2):
        ys_f[k] = cols[12 + k]
        ys_me[k] = jnp.concatenate([cols[14 + 2 * k], cols[15 + 2 * k]], 0).astype(BF16)

    pl.semaphore_wait(barrier, len(greeted))

    started = []

    def send(kind, x_src, x_dst, y_src, y_dst):
        copies = []
        for k, device in enumerate(row_peers):
            copies.append(pltpu.make_async_remote_copy(
                src_ref=x_src.at[k], dst_ref=x_dst.at[k], send_sem=x_send.at[kind, k],
                recv_sem=x_recv.at[kind, k], device_id=device, device_id_type=MESH,
            ))
        for k, device in enumerate(col_peers):
            copies.append(pltpu.make_async_remote_copy(
                src_ref=y_src, dst_ref=y_dst.at[k], send_sem=y_send.at[kind, k],
                recv_sem=y_recv.at[kind, k], device_id=device, device_id_type=MESH,
            ))
        for copy in copies:
            copy.start()
        started.extend(copies)
        return copies

    def arrived(copies):
        for copy in copies:
            copy.wait_recv()

    sent_bf = send(0, xs_bf, xr_bf, ys_bf, yr_bf)
    sent_f = send(1, xs_f, xr_f, ys_f, yr_f)
    sent_me = send(2, xs_me, xr_me, ys_me, yr_me)

    for device in near:
        pl.semaphore_signal(hello.at[0], inc=1, device_id=device, device_id_type=MESH)

    cells = jnp.transpose(jnp.broadcast_to(perf_cell[0], (128, 256)))
    wells = jnp.transpose(jnp.broadcast_to(perf_well[0], (128, 256)))
    prods = jnp.transpose(jnp.broadcast_to(productivity[0], (128, 256)))
    lane_p = iota((256, 128), 1)
    cell_line = cells // 128
    cell_row[:, 0:128] = jnp.where(cell_line == lane_p, 1.0, 0.0).astype(BF16)
    cell_row[:, 128:256] = jnp.where(cell_line == lane_p + 128, 1.0, 0.0).astype(BF16)
    col_weight[...] = jnp.where(cells % 128 == lane_p, prods, 0.0)
    for block in range(2):
        tz[block, nz] = zero
        for buf in (y_a, y_b):
            for c in range(2):
                buf[block, c, 0] = zero
                buf[block, c, nz + 1] = zero

    def get_rows(recv, k, s):
        if recv.dtype == BF16:
            low, high = (recv[d, k, s].astype(F32).reshape(2, 8, 128) for d in range(2))
        else:
            low, high = (recv[d, k, pl.ds(2 * s, 2)] for d in range(2))
        return unpack_rows(low, high)

    def rim(recv, k):
        if recv.dtype == BF16:
            part = [recv[d, k // 2, 0:16].astype(F32)[8 * (k % 2) : 8 * (k % 2) + 8] for d in range(6)]
        else:
            part = [recv[d, k] for d in range(6)]
        beside, up, down = (jnp.where(col_of < 3, part[d], part[d + 1]) for d in (0, 2, 4))
        return beside, jnp.where(sub1 < 4, up, down)

    arrived(sent_bf)

    def rim_trans(s, old):
        at = pl.ds(s * PACK, PACK)
        tx[1, at] = get_rows(xr_bf, 8, s)
        fy = get_rows(xr_bf, 9, s)
        ty[1, at] = fy
        tz[1, at] = get_rows(xr_bf, 10, s)
        for t in range(PACK):
            old = pack_cols(old, fy[t], s * PACK + t)
        return old

    ty_cols = (cols[9], lax.fori_loop(0, packs, rim_trans, zero))
    rim_tx, rim_ty, rim_tz, rim_typ = (rim(yr_bf, k) for k in (8, 9, 10, 11))
    rim_txp = row_shift(*rim_tx, 7)
    rim_all = []
    for block in range(2):
        at_edge = pltpu.roll(ty_cols[block], 127, 1)
        faces = [
            rim_tx[block], rim_txp[block], rim_ty[block],
            jnp.where(col_of == 2, at_edge, rim_typ[block]),
            rim_tz[block], pltpu.roll(rim_tz[block], 128 - WIDE, 1),
        ]
        for k in range(6):
            rim_faces[k, block] = faces[k]
        rim_all.append(faces[0] + faces[1] + faces[2] + faces[3] + faces[4] + faces[5])

    def ends(packed, s):
        return jnp.stack([pltpu.roll(packed, 125 - WIDE * (s * CHUNK + t), 1) for t in range(CHUNK)])

    def faces_late(s, cols):
        cols = [list(c) for c in cols]
        at4 = pl.ds(s * PACK, PACK)
        rim_mob = [get_rows(xr_bf, k, s) for k in range(4)]
        rim_acc = [get_rows(xr_bf, 4 + k, s) for k in range(4)]
        rim_grad = [get_rows(xr_f, c, s) for c in range(2)]
        for h in range(PACK // CHUNK):
            part = slice(h * CHUNK, (h + 1) * CHUNK)
            step = s * (PACK // CHUNK) + h
            at = pl.ds(step * CHUNK, CHUNK)
            after = pl.ds(step * CHUNK + 1, CHUNK)
            lane = iota((CHUNK, 8, 128), 2)
            far_x = row_shift(tx[0, at], tx[1, at], 7)
            for block in range(2):
                fy = ty[block, at]
                far_y = pltpu.roll(jnp.where(lane == 0, ends(rim_ty[block], step), fy), 127, 2)
                txp[block, at] = far_x[block]
                typ[block, at] = far_y
                faces = tx[block, at] + far_x[block] + fy + far_y + tz[block, at] + tz[block, after]
                if block == 0:
                    mob = [mob_late[k, at].astype(F32) for k in range(4)]
                    acc = [accum[k, at].astype(F32) for k in range(4)]
                    grad = [grad_late[c, at] for c in range(2)]
                else:
                    mob, acc, grad = ([x[part] for x in f] for f in (rim_mob, rim_acc, rim_grad))
                inv, mat = block_system(acc, mob, faces)
                for k in range(4):
                    k_late[block, k, at] = mat[k]
                first = transpose_apply(inv, grad)
                for c in range(2):
                    base_late[block, c, at] = first[c]
                    y_a[block, c, after] = first[c]
                    for t in range(CHUNK):
                        cols[block][c] = pack_cols(cols[block][c], first[c][t], step * CHUNK + t)
                if block == 0:
                    mob = [mob_early[k, at].astype(F32) for k in range(4)]
                    inv, mat = block_system(acc, mob, faces)
                    for k in range(4):
                        k_early[0, k, at] = mat[k]
                        inv_early[k, at] = inv[k]
        return tuple(tuple(c) for c in cols)

    arrived(sent_f)
    cols_none = ((zero, zero), (zero, zero))
    late_cols = lax.fori_loop(0, packs, faces_late, cols_none)
    rim_acc_y = [rim(yr_bf, 4 + k) for k in range(4)]
    rim_mob_y = [rim(yr_bf, k) for k in range(4)]
    rim_grad_y = [rim(yr_f, c) for c in range(2)]
    for block in range(2):
        inv, mat = block_system(
            [x[block] for x in rim_acc_y], [x[block] for x in rim_mob_y], rim_all[block], live
        )
        first = transpose_apply(inv, [x[block] for x in rim_grad_y])
        for k in range(4):
            rim_k_late[block, k] = mat[k]
        for c in range(2):
            rim_late[block, c] = first[c]
            rim_a[block, c] = first[c]

    def sweep(cols, y, rim_y, mats, base, rim_mats, rim_base, y_out, rim_out, last=False):
        old = [[rim_y[block, c] for c in range(2)] for block in range(2)]
        blocks = (0,) if last else (0, 1)

        def body(s, packed):
            packed = [list(p) for p in packed]
            at = pl.ds(s * CHUNK, CHUNK)
            at1 = pl.ds(s * CHUNK + 1, CHUNK)
            at2 = pl.ds(s * CHUNK + 2, CHUNK)
            lane = iota((CHUNK, 8, 128), 2)
            flow = [[], []]
            for c in range(2):
                mid = [y[block, c, at1] for block in range(2)]
                below = row_shift(*mid, 1)
                above = row_shift(*mid, 7)
                for block in blocks:
                    side = ends(old[block][c], s)
                    y_low = pltpu.roll(jnp.where(lane == 127, side, mid[block]), 1, 2)
                    y_high = pltpu.roll(jnp.where(lane == 0, side, mid[block]), 127, 2)
                    flow[block].append(
                        tx[block, at] * below[block] + txp[block, at] * above[block]
                        + ty[block, at] * y_low + typ[block, at] * y_high
                        + tz[block, at] * y[block, c, at] + tz[block, at1] * y[block, c, at2]
                    )
            for block in blocks:
                for c in range(2):
                    new = (
                        base[block, c, at] + mats[block, 2 * c, at] * flow[block][0]
                        + mats[block, 2 * c + 1, at] * flow[block][1]
                    )
                    if last:
                        y_out(c, s, new)
                    else:
                        y_out[block, c, at1] = new
                        for t in range(CHUNK):
                            packed[block][c] = pack_cols(packed[block][c], new[t], s * CHUNK + t)
            return tuple(tuple(p) for p in packed)

        packed = lax.fori_loop(0, steps, body, cols_none)
        if last:
            return None
        flow = [[], []]
        for c in range(2):
            below = row_shift(old[0][c], old[1][c], 1)
            above = row_shift(old[0][c], old[1][c], 7)
            for block in range(2):
                mid, own = old[block][c], cols[block][c]
                f = [rim_faces[k, block] for k in range(6)]
                flow[block].append(
                    f[0] * below[block] + f[1] * above[block]
                    + f[2] * pltpu.roll(jnp.where(col_of == 2, own, mid), 1, 1)
                    + f[3] * pltpu.roll(jnp.where(col_of == 3, own, mid), 127, 1)
                    + f[4] * pltpu.roll(mid, WIDE, 1) + f[5] * pltpu.roll(mid, 128 - WIDE, 1)
                )
        for block in range(2):
            for c in range(2):
                rim_out[block, c] = (
                    rim_base[block, c] + rim_mats[block, 2 * c] * flow[block][0]
                    + rim_mats[block, 2 * c + 1] * flow[block][1]
                )
        return packed

    late_args = (k_late, base_late, rim_k_late, rim_late)
    late_cols = sweep(late_cols, y_a, rim_a, *late_args, y_b, rim_b)
    late_cols = sweep(late_cols, y_b, rim_b, *late_args, y_a, rim_a)

    def keep_late(c, s, new):
        y_b[0, c, pl.ds(s * CHUNK + 1, CHUNK)] = new

    sweep(late_cols, y_a, rim_a, *late_args, keep_late, None, last=True)

    def start_early(s, cols):
        cols = list(cols)
        at = pl.ds(s * PACK, PACK)
        at1 = pl.ds(s * PACK + 1, PACK)
        late = [y_b[0, c, at1] for c in range(2)]
        more = transpose_apply([accum[k, at].astype(F32) for k in range(4)], late)
        source = [grad_early[c, at] + more[c] for c in range(2)]
        first = transpose_apply([inv_early[k, at] for k in range(4)], source)
        for c in range(2):
            base_early[0, c, at] = first[c]
            y_a[0, c, at1] = first[c]
            put_rows(first[c], s, xs_e, c)
            for t in range(PACK):
                cols[c] = pack_cols(cols[c], first[c][t], s * PACK + t)
        return tuple(cols)

    own_cols = lax.fori_loop(0, packs, start_early, (zero, zero))
    for c in range(2):
        ys_e[c] = own_cols[c]
    sent_e = send(3, xs_e, xr_e, ys_e, yr_e)

    pl.semaphore_wait(hello.at[0], len(near))
    for device in far:
        pl.semaphore_signal(hello.at[1], inc=1, device_id=device, device_id_type=MESH)
    arrived(sent_me)

    def rim_early_mats(s, _):
        rim_mob = [get_rows(xr_me, k, s) for k in range(4)]
        rim_acc = [get_rows(xr_bf, 4 + k, s) for k in range(4)]
        at = pl.ds(s * PACK, PACK)
        after = pl.ds(s * PACK + 1, PACK)
        faces = tx[1, at] + txp[1, at] + ty[1, at] + typ[1, at] + tz[1, at] + tz[1, after]
        _, mat = block_system(rim_acc, rim_mob, faces)
        for k in range(4):
            k_early[1, k, at] = mat[k]
        return 0

    lax.fori_loop(0, packs, rim_early_mats, 0)
    rim_mob_y = [rim(yr_me, k) for k in range(4)]
    for block in range(2):
        _, mat = block_system(
            [x[block] for x in rim_acc_y], [x[block] for x in rim_mob_y], rim_all[block], live
        )
        for k in range(4):
            rim_k_early[block, k] = mat[k]

    pad = jnp.zeros((256 - 8 * nz, 128), F32)

    def picked(field):
        lines = jnp.concatenate([field.reshape(8 * nz, 128), pad], 0)
        terms = onehot_dot(cell_row[...], lines) * col_weight[...]
        return jnp.sum(terms, axis=1, keepdims=True)

    own_lane = lane_p - wells % 8
    spread = jnp.zeros((256, 128), F32)
    for c in range(2):
        spread = jnp.where(own_lane == 8 * (c + 2), picked(y_b[0, c, pl.ds(1, nz)]), spread)
    owner = jnp.where(
        iota((n_gx, 256), 0) == jnp.broadcast_to(perf_well[0] // 8, (n_gx, 256)), 1.0, 0.0
    ).astype(BF16)

    arrived(sent_e)

    def rim_start(s, cols):
        cols = list(cols)
        at = pl.ds(s * PACK, PACK)
        at1 = pl.ds(s * PACK + 1, PACK)
        for c in range(2):
            first = get_rows(xr_e, c, s)
            base_early[1, c, at] = first
            y_a[1, c, at1] = first
            for t in range(PACK):
                cols[c] = pack_cols(cols[c], first[t], s * PACK + t)
        return tuple(cols)

    early_cols = (own_cols, lax.fori_loop(0, packs, rim_start, (zero, zero)))
    for c in range(2):
        pair = rim(yr_e, c)
        for block in range(2):
            rim_early[block, c] = pair[block]
            rim_a[block, c] = pair[block]

    early_args = (k_early, base_early, rim_k_early, rim_early)
    early_cols = sweep(early_cols, y_a, rim_a, *early_args, y_b, rim_b)
    early_cols = sweep(early_cols, y_b, rim_b, *early_args, y_a, rim_a)

    def keep_early(c, s, new):
        early_out[c, pl.ds(s * CHUNK, CHUNK)] = new

    sweep(early_cols, y_a, rim_a, *early_args, keep_early, None, last=True)

    for c in range(2):
        spread = jnp.where(own_lane == 8 * c, picked(early_out[c]), spread)
    partial = onehot_dot(owner, spread)
    for o in range(n_gx):
        pbuf[o] = partial[o : o + 1]

    for d in range(1, a_count):
        t, device = a_partner(d)
        copy = pltpu.make_async_remote_copy(
            src_ref=pbuf.at[pl.ds(t * per_dev, per_dev)], dst_ref=ra.at[pl.ds(d * per_dev, per_dev)],
            send_sem=a_send.at[d], recv_sem=a_recv, device_id=device, device_id_type=MESH,
        )
        copy.start()
        started.append(copy)
    landed = ra.at[pl.ds(per_dev, n_gx - per_dev)]
    pltpu.make_async_copy(landed, landed, a_recv).wait()
    for r in range(per_dev):
        total = pbuf[q * per_dev + r]
        for d in range(1, a_count):
            total = total + ra[d * per_dev + r]
        sb[r] = total

    pl.semaphore_wait(hello.at[1], len(far))

    def b_copy(r, dest_j):
        dest_i = q * per_dev + r
        own = jnp.logical_and(dest_i == i, j == dest_j)
        return own, pltpu.make_async_remote_copy(
            src_ref=sb.at[r], dst_ref=rb.at[plane], send_sem=b_send.at[r * n_gy + dest_j], recv_sem=b_recv,
            device_id=(dest_i, dest_j), device_id_type=MESH,
        )

    for r in range(per_dev):
        for dest_j in range(n_gy):
            own, copy = b_copy(r, dest_j)
            pl.when(jnp.logical_not(own))(copy.start)
            pl.when(own)(pltpu.make_async_copy(sb.at[r], rb.at[plane], b_recv).start)
    pltpu.make_async_copy(rb, rb, b_recv).wait()
    total = rb[0]
    for p in range(1, planes):
        total = total + rb[p]
    total = jnp.broadcast_to(total, (8, 128))
    out = total
    for k in range(1, 4):
        out = jnp.where(sub1 == k, pltpu.roll(total, 128 - 8 * k, 1), out)
    wells_out[...] = out[0:4, 0:8]

    for copy in started:
        copy.wait_send()
    for r in range(per_dev):
        for dest_j in range(n_gy):
            own, copy = b_copy(r, dest_j)
            pl.when(jnp.logical_not(own))(copy.wait_send)


def per_device(n_gx, n_gy, *args):
    nz = args[5].shape[0]
    a_count = 4 * n_gy
    per_dev = n_gx // a_count
    planes = n_gx // 4
    packs = nz // PACK

    def f32(*lead):
        return pltpu.VMEM((*lead, 8, 128), F32)

    def bf16(*lead):
        return pltpu.VMEM((*lead, 16, 128), BF16)

    dma = pltpu.SemaphoreType.DMA
    vmem = pl.BlockSpec(memory_space=pltpu.VMEM)
    return pl.pallas_call(
        functools.partial(kernel, n_gx, n_gy, nz),
        out_shape=(
            jax.ShapeDtypeStruct((2, nz, 8, 128), F32),
            jax.ShapeDtypeStruct((4, 8), F32),
        ),
        in_specs=[pl.BlockSpec(memory_space=pltpu.HBM)] * 11,
        out_specs=(vmem, vmem),
        scratch_shapes=[pltpu.VMEM(a.shape, a.dtype) for a in args] + [
            dma((11,)),
            f32(2, nz), f32(2, nz), f32(2, nz), f32(2, nz), f32(2, nz + 1),
            f32(2, 4, nz), f32(2, 4, nz), f32(4, nz), f32(2, 2, nz), f32(2, 2, nz),
            f32(2, 2, nz + 2), f32(2, 2, nz + 2),
            f32(6, 2), f32(2, 4), f32(2, 4), f32(2, 2), f32(2, 2), f32(2, 2), f32(2, 2),
            bf16(2, 11, packs), f32(2, 2, 2 * packs), bf16(2, 4, packs), f32(2, 2, 2 * packs),
            bf16(2, 11, packs), f32(2, 2, 2 * packs), bf16(2, 4, packs), f32(2, 2, 2 * packs),
            dma((4, 2)), dma((4, 2)),
            bf16(6), f32(2), bf16(2), f32(2),
            bf16(6, 6), f32(6, 2), bf16(6, 2), f32(6, 2),
            dma((4, 6)), dma((4, 6)),
            pltpu.VMEM((256, 256), BF16), pltpu.VMEM((256, 128), F32),
            pltpu.VMEM((n_gx, 1, 128), F32), pltpu.VMEM((n_gx, 1, 128), F32),
            pltpu.VMEM((per_dev, 1, 128), F32), pltpu.VMEM((planes, 1, 128), F32),
            dma((a_count,)), dma, dma((per_dev * n_gy,)), dma,
            pltpu.SemaphoreType.REGULAR((2,)),
        ],
        compiler_params=pltpu.CompilerParams(
            collective_id=0, has_side_effects=True, vmem_limit_bytes=60 * 1024 * 1024
        ),
    )(*args)


def solution(mesh):
    n_gx, n_gy = mesh.shape["gx"], mesh.shape["gy"]
    cells = P(None, None, "gx", "gy")
    faces = P(None, "gx", "gy")
    perfs = P("gx", "gy", None)
    return jax.shard_map(
        functools.partial(per_device, n_gx, n_gy),
        mesh=mesh,
        in_specs=(cells,) * 5 + (faces,) * 3 + (perfs,) * 3,
        out_specs=(cells, P(None, "gx")),
        check_vma=False,
    )
```

time: 72.9 us -> 65.8 us (0.903)
  Pallas kernels: 69.9 us -> 62.9 us
    pallas_call x1, Pallas kernels: 69.9 us -> 62.9 us  [per_device(): pl.pallas_call(functools.partial(kernel, n_gx, n_gy, nz), out_shape=(jax....]
where the time goes in v3:
time: 65.8 us; the launch traced here: 65.7 us
  Pallas kernels  62.9 us (96%)
  local copies, waits for them, and re-layouts  2.18 us (3%)
    pallas_call x1, Pallas kernels, per_device(): pl.pallas_call(functools.partial(kernel, n_gx, n_gy, nz), out_shape=(jax....  62.9 us
    unnamed x4, local copies, waits for them, and re-layouts  2.18 us

profile of v3, /device:TPU:1, one launch (start us, length us, event | category | flops | bytes accessed | tf_op | source)
XLA Modules:
  0.0 65.7 jit_solution(17009042385233650245)
XLA Ops:
  0.6 62.9 %shard_map.122 = (f32[2,20,8,128]{3,2,1,0:T(8,128)}, f32[4,8]{1,0:T(4,128)}) custom-call(f32[2,20,8,128]{3,2,1,0:T(8,128)} %refs_0_.1, f32[2,20,8,128]{3,2,1,0:T(8,128)} %refs_1_.1, bf16[4,20,8,128]{3,2,1,0:T(8,128)(2,1)} %refs_2_.1, bf16[4,20,8,128]{3,2,1,0:T(8,128)(2,1)} %refs_3_.1, bf16[4,20,8,128]{3,2,1,0:T(8,128)(2,1)} %refs_4_.1, ...), custom_call_target="tpu_custom_call" | custom-call | tf_op jit(solution)/shard_map/pallas_call | solution.py:563
  63.5 0.0 copy-start
  63.5 1.6 %copy.15 = f32[2,20,8,128]{3,2,1,0:T(8,128)} copy(f32[2,20,8,128]{3,2,1,0:T(8,128)} %get-tuple-element.4) | data formatting | bytes 327680
  65.1 0.0 copy-done
  65.1 0.6 copy.16
Async XLA Ops:
  63.5 1.6 %copy-start = (f32[4,8]{1,0:T(4,128)S(1)}, f32[4,8]{1,0:T(4,128)}, u32[]{:S(2)}) copy-start(f32[4,8]{1,0:T(4,128)} %get-tuple-element.5) | copy-start | bytes 388

commit v4 on v3

--- a/solution.py
+++ b/solution.py
@@ -170,7 +170,7 @@
                 cols[k] = pack_cols(cols[k], x[t], layer, 2 if k == 11 else 3)
         return tuple(cols)
 
-    cols = lax.fori_loop(0, packs, first_out, (zero,) * 18)
+    cols = lax.fori_loop(0, packs, first_out, (zero,) * 18, unroll=5)
     for k in range(6):
         ys_bf[k] = jnp.concatenate([cols[2 * k], cols[2 * k + 1]], 0).astype(BF16)
     for k in range(2):
@@ -251,7 +251,7 @@
             old = pack_cols(old, fy[t], s * PACK + t)
         return old
 
-    ty_cols = (cols[9], lax.fori_loop(0, packs, rim_trans, zero))
+    ty_cols = (cols[9], lax.fori_loop(0, packs, rim_trans, zero, unroll=5))
     rim_tx, rim_ty, rim_tz, rim_typ = (rim(yr_bf, k) for k in (8, 9, 10, 11))
     rim_txp = row_shift(*rim_tx, 7)
     rim_all = []
@@ -313,7 +313,7 @@
 
     arrived(sent_f)
     cols_none = ((zero, zero), (zero, zero))
-    late_cols = lax.fori_loop(0, packs, faces_late, cols_none)
+    late_cols = lax.fori_loop(0, packs, faces_late, cols_none, unroll=5)
     rim_acc_y = [rim(yr_bf, 4 + k) for k in range(4)]
     rim_mob_y = [rim(yr_bf, k) for k in range(4)]
     rim_grad_y = [rim(yr_f, c) for c in range(2)]
@@ -366,7 +366,7 @@
                             packed[block][c] = pack_cols(packed[block][c], new[t], s * CHUNK + t)
             return tuple(tuple(p) for p in packed)
 
-        packed = lax.fori_loop(0, steps, body, cols_none)
+        packed = lax.fori_loop(0, steps, body, cols_none, unroll=5)
         if last:
             return None
         flow = [[], []]
@@ -415,7 +415,7 @@
                 cols[c] = pack_cols(cols[c], first[c][t], s * PACK + t)
         return tuple(cols)
 
-    own_cols = lax.fori_loop(0, packs, start_early, (zero, zero))
+    own_cols = lax.fori_loop(0, packs, start_early, (zero, zero), unroll=5)
     for c in range(2):
         ys_e[c] = own_cols[c]
     sent_e = send(3, xs_e, xr_e, ys_e, yr_e)
@@ -436,7 +436,7 @@
             k_early[1, k, at] = mat[k]
         return 0
 
-    lax.fori_loop(0, packs, rim_early_mats, 0)
+    lax.fori_loop(0, packs, rim_early_mats, 0, unroll=5)
     rim_mob_y = [rim(yr_me, k) for k in range(4)]
     for block in range(2):
         _, mat = block_system(
@@ -474,7 +474,7 @@
                 cols[c] = pack_cols(cols[c], first[t], s * PACK + t)
         return tuple(cols)
 
-    early_cols = (own_cols, lax.fori_loop(0, packs, rim_start, (zero, zero)))
+    early_cols = (own_cols, lax.fori_loop(0, packs, rim_start, (zero, zero), unroll=5))
     for c in range(2):
         pair = rim(yr_e, c)
         for block in range(2):

time: 65.8 us -> 56.8 us (0.86)
  Pallas kernels: 62.9 us -> 53.8 us
    pallas_call x1, Pallas kernels: 62.9 us -> 53.8 us  [per_device(): pl.pallas_call(functools.partial(kernel, n_gx, n_gy, nz), out_shape=(jax....]
where the time goes in v4:
time: 56.8 us; the launch traced here: 56.7 us
  Pallas kernels  53.8 us (95%)
  local copies, waits for them, and re-layouts  2.18 us (4%)
  between operations  0.65 us (1%)
    pallas_call x1, Pallas kernels, per_device(): pl.pallas_call(functools.partial(kernel, n_gx, n_gy, nz), out_shape=(jax....  53.8 us
    unnamed x4, local copies, waits for them, and re-layouts  2.18 us

profile of v4, /device:TPU:1, one launch (start us, length us, event | category | flops | bytes accessed | tf_op | source)
XLA Modules:
  0.0 56.7 jit_solution(5442402169733081279)
XLA Ops:
  0.6 53.8 %shard_map.122 = (f32[2,20,8,128]{3,2,1,0:T(8,128)}, f32[4,8]{1,0:T(4,128)}) custom-call(f32[2,20,8,128]{3,2,1,0:T(8,128)} %refs_0_.1, f32[2,20,8,128]{3,2,1,0:T(8,128)} %refs_1_.1, bf16[4,20,8,128]{3,2,1,0:T(8,128)(2,1)} %refs_2_.1, bf16[4,20,8,128]{3,2,1,0:T(8,128)(2,1)} %refs_3_.1, bf16[4,20,8,128]{3,2,1,0:T(8,128)(2,1)} %refs_4_.1, ...), custom_call_target="tpu_custom_call" | custom-call | tf_op jit(solution)/shard_map/pallas_call | solution.py:563
  54.5 0.0 copy-start
  54.5 1.6 %copy.15 = f32[2,20,8,128]{3,2,1,0:T(8,128)} copy(f32[2,20,8,128]{3,2,1,0:T(8,128)} %get-tuple-element.4) | data formatting | bytes 327680
  56.1 0.0 copy-done
  56.1 0.6 %copy.16 = f32[4,8]{1,0:T(4,128)} copy(f32[4,8]{1,0:T(4,128)S(1)} %copy-done) | data formatting | bytes 256
Async XLA Ops:
  54.5 1.6 %copy-start = (f32[4,8]{1,0:T(4,128)S(1)}, f32[4,8]{1,0:T(4,128)}, u32[]{:S(2)}) copy-start(f32[4,8]{1,0:T(4,128)} %get-tuple-element.5) | copy-start | bytes 388

commit v5 on v4

--- a/solution.py
+++ b/solution.py
@@ -79,6 +79,7 @@
         rim_faces, rim_k_late, rim_k_early, rim_late, rim_early, rim_a, rim_b,
         xs_bf, xs_f, xs_me, xs_e, xr_bf, xr_f, xr_me, xr_e, x_send, x_recv,
         ys_bf, ys_f, ys_me, ys_e, yr_bf, yr_f, yr_me, yr_e, y_send, y_recv,
+        zs_bf, zs_f, zs_e, zr_bf, zr_f, zr_e, z_send, z_recv,
         cell_row, col_weight, pbuf, ra, sb, rb, a_send, a_recv, b_send, b_recv, hello,
     ) = refs[24:]
     (
@@ -96,11 +97,19 @@
     lower, upper = (i + n_gx - 1) % n_gx, (i + 1) % n_gx
     left, right = (j + n_gy - 1) % n_gy, (j + 1) % n_gy
     row_peers = ((upper, j), (lower, j))
-    col_peers = ((i, right), (i, left), (lower, right), (lower, left), (upper, right), (upper, left))
+    col_peers = ((i, right), (i, left))
+    corner_peers = ((upper, right), (upper, left), (lower, right), (lower, left))
+    px, py, core = 2 * (j % 2) + spot // 2, j // 2, spot % 2
+    offsets = sorted(
+        ((dx, dy, dc) for dx in range(4) for dy in range(4) for dc in range(2)),
+        key=lambda o: -min(o[0], 4 - o[0]) - min(o[1], 4 - o[1]) - o[2] / 2,
+    )
 
     def a_partner(d):
-        t = (q + d) % a_count
-        return t, (plane * group + t // n_gy, t % n_gy)
+        dx, dy, dc = offsets[d]
+        x, to_core = (px + dx) % 4, core + dc - 2 * core * dc
+        to_j, to_spot = ((py + dy) % 4) * 2 + x // 2, (x % 2) * 2 + to_core
+        return to_spot * n_gy + to_j, (plane * group + to_spot, to_j)
 
     loads = [
         pltpu.make_async_copy(inputs[k], held[k], in_sem.at[k])
@@ -115,7 +124,7 @@
     near = [mate(d) for d in (-3, -2, -1, 1, 2, 3)]
     far = [mate(d) for d in (-5, 5)]
     barrier = pltpu.get_barrier_semaphore()
-    greeted = [*row_peers, *col_peers, *near] + [a_partner(d)[1] for d in range(1, a_count)]
+    greeted = [*row_peers, *col_peers, *corner_peers, *near] + [a_partner(d)[1] for d in range(a_count - 1)]
     for device in greeted:
         pl.semaphore_signal(barrier, inc=1, device_id=device, device_id_type=MESH)
     for load in loads:
@@ -171,40 +180,60 @@
         return tuple(cols)
 
     cols = lax.fori_loop(0, packs, first_out, (zero,) * 18, unroll=5)
-    for k in range(6):
-        ys_bf[k] = jnp.concatenate([cols[2 * k], cols[2 * k + 1]], 0).astype(BF16)
-    for k in range(2):
-        ys_f[k] = cols[12 + k]
-        ys_me[k] = jnp.concatenate([cols[14 + 2 * k], cols[15 + 2 * k]], 0).astype(BF16)
+    def pair_cols(a, b):
+        return (
+            jnp.where(col_of < 3, a, pltpu.roll(b, 3, 1)),
+            jnp.where(col_of < 3, pltpu.roll(a, 125, 1), b),
+        )
+
+    def pair_corners(p, r):
+        turned = pltpu.roll(r, 4, 0)
+        return jnp.where(sub1 < 4, turned, p), jnp.where(sub1 < 4, p, turned)
+
+    def to_bf(a, b):
+        return jnp.concatenate([a, b], 0).astype(BF16)
+
+    pairs = [pair_cols(cols[2 * k], cols[2 * k + 1]) for k in range(9)]
+    for side in range(2):
+        part = [p[side] for p in pairs]
+        for k in range(3):
+            ys_bf[side, k] = to_bf(part[2 * k], part[2 * k + 1])
+        ys_f[side] = part[6]
+        ys_me[side] = to_bf(part[7], part[8])
+        order = (0, 1, 2, 3, 4, 5, 7, 8)
+        quads = [pair_corners(part[order[2 * k]], part[order[2 * k + 1]]) for k in range(4)]
+        for end in range(2):
+            for k in range(2):
+                zs_bf[2 * end + side, k] = to_bf(quads[2 * k][end], quads[2 * k + 1][end])
+            zs_f[2 * end + side] = part[6]
 
     pl.semaphore_wait(barrier, len(greeted))
 
     started = []
 
-    def send(kind, x_src, x_dst, y_src, y_dst):
+    def send(kind, *parts):
         copies = []
-        for k, device in enumerate(row_peers):
-            copies.append(pltpu.make_async_remote_copy(
-                src_ref=x_src.at[k], dst_ref=x_dst.at[k], send_sem=x_send.at[kind, k],
-                recv_sem=x_recv.at[kind, k], device_id=device, device_id_type=MESH,
-            ))
-        for k, device in enumerate(col_peers):
-            copies.append(pltpu.make_async_remote_copy(
-                src_ref=y_src, dst_ref=y_dst.at[k], send_sem=y_send.at[kind, k],
-                recv_sem=y_recv.at[kind, k], device_id=device, device_id_type=MESH,
-            ))
+        for src, dst, peers, sems in parts:
+            for k, device in enumerate(peers):
+                copies.append(pltpu.make_async_remote_copy(
+                    src_ref=src.at[k], dst_ref=dst.at[k], send_sem=sems[0].at[kind, k],
+                    recv_sem=sems[1].at[kind, k], device_id=device, device_id_type=MESH,
+                ))
         for copy in copies:
             copy.start()
         started.extend(copies)
         return copies
 
+    rows = row_peers, (x_send, x_recv)
+    sides = col_peers, (y_send, y_recv)
+    corners = corner_peers, (z_send, z_recv)
+
     def arrived(copies):
         for copy in copies:
             copy.wait_recv()
 
-    sent_bf = send(0, xs_bf, xr_bf, ys_bf, yr_bf)
-    sent_f = send(1, xs_f, xr_f, ys_f, yr_f)
-    sent_me = send(2, xs_me, xr_me, ys_me, yr_me)
+    sent_bf = send(0, (xs_bf, xr_bf, *rows), (zs_bf, zr_bf, *corners), (ys_bf, yr_bf, *sides))
+    sent_f = send(1, (xs_f, xr_f, *rows), (zs_f, zr_f, *corners), (ys_f, yr_f, *sides))
 
     for device in near:
         pl.semaphore_signal(hello.at[0], inc=1, device_id=device, device_id_type=MESH)
@@ -231,13 +260,36 @@
             low, high = (recv[d, k, pl.ds(2 * s, 2)] for d in range(2))
         return unpack_rows(low, high)
 
-    def rim(recv, k):
-        if recv.dtype == BF16:
-            part = [recv[d, k // 2, 0:16].astype(F32)[8 * (k % 2) : 8 * (k % 2) + 8] for d in range(6)]
-        else:
-            part = [recv[d, k] for d in range(6)]
-        beside, up, down = (jnp.where(col_of < 3, part[d], part[d + 1]) for d in (0, 2, 4))
-        return beside, jnp.where(sub1 < 4, up, down)
+    def split_cols(a, b):
+        return (
+            jnp.where(col_of < 3, a, pltpu.roll(b, 3, 1)),
+            jnp.where(col_of < 3, pltpu.roll(a, 125, 1), b),
+        )
+
+    def halves(tile):
+        tile = tile.astype(F32)
+        return tile[0:8], tile[8:16]
+
+    def split_rows(down, up):
+        return jnp.where(sub1 < 4, up, down), pltpu.roll(jnp.where(sub1 < 4, down, up), 4, 0)
+
+    def rim_fields(y_tiles, z_tiles):
+        beside = [split_cols(*pair) for pair in zip(*y_tiles)]
+        corner = [split_cols(*pair) for pair in zip(*z_tiles)]
+        return [(beside[k // 2][k % 2], corner[k // 2][k % 2]) for k in range(2 * len(beside))]
+
+    def corner_bf(quads):
+        tiles = []
+        for side in range(2):
+            part = []
+            for k in quads:
+                down, up = (halves(zr_bf[d + side, k // 2])[k % 2] for d in (0, 2))
+                part += split_rows(down, up)
+            tiles.append(part)
+        return tiles
+
+    def corner_f(recv):
+        return [[jnp.where(sub1 < 4, recv[2 + side], recv[side])] for side in range(2)]
 
     arrived(sent_bf)
 
@@ -252,7 +304,11 @@
         return old
 
     ty_cols = (cols[9], lax.fori_loop(0, packs, rim_trans, zero, unroll=5))
-    rim_tx, rim_ty, rim_tz, rim_typ = (rim(yr_bf, k) for k in (8, 9, 10, 11))
+    rim_bf = rim_fields(
+        [[h for k in range(3) for h in halves(yr_bf[side, k])] for side in range(2)],
+        corner_bf((0, 1, 2)),
+    )
+    rim_tx, rim_ty, rim_tz, rim_typ = rim_bf[8:12]
     rim_txp = row_shift(*rim_tx, 7)
     rim_all = []
     for block in range(2):
@@ -312,11 +368,11 @@
         return tuple(tuple(c) for c in cols)
 
     arrived(sent_f)
+    sent_me = send(2, (xs_me, xr_me, *rows), (ys_me, yr_me, *sides))
     cols_none = ((zero, zero), (zero, zero))
     late_cols = lax.fori_loop(0, packs, faces_late, cols_none, unroll=5)
-    rim_acc_y = [rim(yr_bf, 4 + k) for k in range(4)]
-    rim_mob_y = [rim(yr_bf, k) for k in range(4)]
-    rim_grad_y = [rim(yr_f, c) for c in range(2)]
+    rim_mob_y, rim_acc_y = rim_bf[0:4], rim_bf[4:8]
+    rim_grad_y = rim_fields([[yr_f[side]] for side in range(2)], corner_f(zr_f))
     for block in range(2):
         inv, mat = block_system(
             [x[block] for x in rim_acc_y], [x[block] for x in rim_mob_y], rim_all[block], live
@@ -416,9 +472,12 @@
         return tuple(cols)
 
     own_cols = lax.fori_loop(0, packs, start_early, (zero, zero), unroll=5)
-    for c in range(2):
-        ys_e[c] = own_cols[c]
-    sent_e = send(3, xs_e, xr_e, ys_e, yr_e)
+    pair = pair_cols(*own_cols)
+    for side in range(2):
+        ys_e[side] = pair[side]
+        for end in range(2):
+            zs_e[2 * end + side] = pair[side]
+    sent_e = send(3, (xs_e, xr_e, *rows), (zs_e, zr_e, *corners), (ys_e, yr_e, *sides))
 
     pl.semaphore_wait(hello.at[0], len(near))
     for device in far:
@@ -437,7 +496,7 @@
         return 0
 
     lax.fori_loop(0, packs, rim_early_mats, 0, unroll=5)
-    rim_mob_y = [rim(yr_me, k) for k in range(4)]
+    rim_mob_y = rim_fields([halves(yr_me[side]) for side in range(2)], corner_bf((3,)))
     for block in range(2):
         _, mat = block_system(
             [x[block] for x in rim_acc_y], [x[block] for x in rim_mob_y], rim_all[block], live
@@ -475,8 +534,9 @@
         return tuple(cols)
 
     early_cols = (own_cols, lax.fori_loop(0, packs, rim_start, (zero, zero), unroll=5))
+    rim_first = rim_fields([[yr_e[side]] for side in range(2)], corner_f(zr_e))
     for c in range(2):
-        pair = rim(yr_e, c)
+        pair = rim_first[c]
         for block in range(2):
             rim_early[block, c] = pair[block]
             rim_a[block, c] = pair[block]
@@ -496,7 +556,7 @@
     for o in range(n_gx):
         pbuf[o] = partial[o : o + 1]
 
-    for d in range(1, a_count):
+    for d in range(a_count - 1):
         t, device = a_partner(d)
         copy = pltpu.make_async_remote_copy(
             src_ref=pbuf.at[pl.ds(t * per_dev, per_dev)], dst_ref=ra.at[pl.ds(d * per_dev, per_dev)],
@@ -504,11 +564,11 @@
         )
         copy.start()
         started.append(copy)
-    landed = ra.at[pl.ds(per_dev, n_gx - per_dev)]
+    landed = ra.at[pl.ds(0, n_gx - per_dev)]
     pltpu.make_async_copy(landed, landed, a_recv).wait()
     for r in range(per_dev):
         total = pbuf[q * per_dev + r]
-        for d in range(1, a_count):
+        for d in range(a_count - 1):
             total = total + ra[d * per_dev + r]
         sb[r] = total
 
@@ -563,8 +623,8 @@
     return pl.pallas_call(
         functools.partial(kernel, n_gx, n_gy, nz),
         out_shape=(
-            jax.ShapeDtypeStruct((2, nz, 8, 128), F32),
-            jax.ShapeDtypeStruct((4, 8), F32),
+            pltpu.VMEM((2, nz, 8, 128), F32),
+            pltpu.VMEM((4, 8), F32),
         ),
         in_specs=[pl.BlockSpec(memory_space=pltpu.HBM)] * 11,
         out_specs=(vmem, vmem),
@@ -577,9 +637,11 @@
             bf16(2, 11, packs), f32(2, 2, 2 * packs), bf16(2, 4, packs), f32(2, 2, 2 * packs),
             bf16(2, 11, packs), f32(2, 2, 2 * packs), bf16(2, 4, packs), f32(2, 2, 2 * packs),
             dma((4, 2)), dma((4, 2)),
-            bf16(6), f32(2), bf16(2), f32(2),
-            bf16(6, 6), f32(6, 2), bf16(6, 2), f32(6, 2),
-            dma((4, 6)), dma((4, 6)),
+            bf16(2, 3), f32(2), bf16(2), f32(2),
+            bf16(2, 3), f32(2), bf16(2), f32(2),
+            dma((4, 2)), dma((4, 2)),
+            bf16(4, 2), f32(4), f32(4), bf16(4, 2), f32(4), f32(4),
+            dma((4, 4)), dma((4, 4)),
             pltpu.VMEM((256, 256), BF16), pltpu.VMEM((256, 128), F32),
             pltpu.VMEM((n_gx, 1, 128), F32), pltpu.VMEM((n_gx, 1, 128), F32),
             pltpu.VMEM((per_dev, 1, 128), F32), pltpu.VMEM((planes, 1, 128), F32),

time: 56.8 us -> 52.4 us (0.923)
  Pallas kernels: 53.8 us -> 50.4 us
  local copies, waits for them, and re-layouts: 2.18 us -> 1.25 us
    pallas_call x1, Pallas kernels: 53.8 us -> 50.4 us  [per_device(): pl.pallas_call(functools.partial(kernel, n_gx, n_gy, nz), out_shape=(pltp...]
    unnamed x4 -> x2, local copies, waits for them, and re-layouts: 2.18 us -> 1.25 us
where the time goes in v5:
time: 52.4 us; the launch traced here: 52.3 us
  Pallas kernels  50.4 us (96%)
  local copies, waits for them, and re-layouts  1.25 us (2%)
  between operations  0.64 us (1%)
    pallas_call x1, Pallas kernels, per_device(): pl.pallas_call(functools.partial(kernel, n_gx, n_gy, nz), out_shape=(pltp...  50.4 us
    unnamed x2, local copies, waits for them, and re-layouts  1.25 us

profile of v5, /device:TPU:1, one launch (start us, length us, event | category | flops | bytes accessed | tf_op | source)
XLA Modules:
  0.0 52.3 jit_solution(7139328344638424193)
XLA Ops:
  0.6 50.4 %shard_map.122 = (f32[2,20,8,128]{3,2,1,0:T(8,128)S(1)}, f32[4,8]{1,0:T(4,128)S(1)}) custom-call(f32[2,20,8,128]{3,2,1,0:T(8,128)} %refs_0_.1, f32[2,20,8,128]{3,2,1,0:T(8,128)} %refs_1_.1, bf16[4,20,8,128]{3,2,1,0:T(8,128)(2,1)} %refs_2_.1, bf16[4,20,8,128]{3,2,1,0:T(8,128)(2,1)} %refs_3_.1, bf16[4,20,8,128]{3,2,1,0:T(8,128)(2,1)} %refs_4_.1, ...), custom_call_target="tpu_custom_call" | custom-call | tf_op jit(solution)/shard_map/pallas_call | solution.py:623
  51.0 0.7 %copy.15 = f32[2,20,8,128]{3,2,1,0:T(8,128)} copy(f32[2,20,8,128]{3,2,1,0:T(8,128)S(1)} %get-tuple-element.2) | data formatting | bytes 327680
  51.7 0.6 %copy.16 = f32[4,8]{1,0:T(4,128)} copy(f32[4,8]{1,0:T(4,128)S(1)} %get-tuple-element.3) | data formatting | bytes 256

commit v6 on v5

--- a/solution.py
+++ b/solution.py
@@ -77,7 +77,7 @@
     (
         in_sem, tx, txp, ty, typ, tz, k_late, k_early, inv_early, base_late, base_early, y_a, y_b,
         rim_faces, rim_k_late, rim_k_early, rim_late, rim_early, rim_a, rim_b,
-        xs_bf, xs_f, xs_me, xs_e, xr_bf, xr_f, xr_me, xr_e, x_send, x_recv,
+        xs_t, xs_bf, xs_f, xs_me, xs_e, xr_t, xr_bf, xr_f, xr_me, xr_e, x_send, x_recv,
         ys_bf, ys_f, ys_me, ys_e, yr_bf, yr_f, yr_me, yr_e, y_send, y_recv,
         zs_bf, zs_f, zs_e, zr_bf, zr_f, zr_e, z_send, z_recv,
         cell_row, col_weight, pbuf, ra, sb, rb, a_send, a_recv, b_send, b_recv, hello,
@@ -89,11 +89,8 @@
     i = lax.axis_index("gx")
     j = lax.axis_index("gy")
     group = 4
-    a_count = group * n_gy
-    per_dev = n_gx // a_count
     planes = n_gx // group
     plane, spot = i // group, i % group
-    q = spot * n_gy + j
     lower, upper = (i + n_gx - 1) % n_gx, (i + 1) % n_gx
     left, right = (j + n_gy - 1) % n_gy, (j + 1) % n_gy
     row_peers = ((upper, j), (lower, j))
@@ -103,13 +100,15 @@
     offsets = sorted(
         ((dx, dy, dc) for dx in range(4) for dy in range(4) for dc in range(2)),
         key=lambda o: -min(o[0], 4 - o[0]) - min(o[1], 4 - o[1]) - o[2] / 2,
-    )
-
-    def a_partner(d):
-        dx, dy, dc = offsets[d]
+    )[:-1]
+
+    def plane_partner(offset):
+        dx, dy, dc = offset
         x, to_core = (px + dx) % 4, core + dc - 2 * core * dc
-        to_j, to_spot = ((py + dy) % 4) * 2 + x // 2, (x % 2) * 2 + to_core
-        return to_spot * n_gy + to_j, (plane * group + to_spot, to_j)
+        to_spot = (x % 2) * 2 + to_core
+        return plane * group + to_spot, ((py + dy) % 4) * 2 + x // 2
+
+    plane_partners = [plane_partner(o) for o in offsets]
 
     loads = [
         pltpu.make_async_copy(inputs[k], held[k], in_sem.at[k])
@@ -124,7 +123,7 @@
     near = [mate(d) for d in (-3, -2, -1, 1, 2, 3)]
     far = [mate(d) for d in (-5, 5)]
     barrier = pltpu.get_barrier_semaphore()
-    greeted = [*row_peers, *col_peers, *corner_peers, *near] + [a_partner(d)[1] for d in range(a_count - 1)]
+    greeted = [*row_peers, *col_peers, *corner_peers, *near] + plane_partners
     for device in greeted:
         pl.semaphore_signal(barrier, inc=1, device_id=device, device_id_type=MESH)
     for load in loads:
@@ -163,9 +162,12 @@
         ty[0, at] = fy
         tz[0, at] = fz
         fields = [mob_late[k, at].astype(F32) for k in range(4)]
-        fields += [accum[k, at].astype(F32) for k in range(4)] + [fx, fy, fz]
+        fields += [accum[k, at].astype(F32) for k in range(4)]
         for k, x in enumerate(fields):
             put_rows(x, s, xs_bf, k)
+        fields += [fx, fy, fz]
+        for k, x in enumerate(fields[8:]):
+            put_rows(x, s, xs_t, k)
         grads = [grad_late[c, at] for c in range(2)]
         for k, x in enumerate(grads):
             put_rows(x, s, xs_f, k)
@@ -232,8 +234,9 @@
         for copy in copies:
             copy.wait_recv()
 
-    sent_bf = send(0, (xs_bf, xr_bf, *rows), (zs_bf, zr_bf, *corners), (ys_bf, yr_bf, *sides))
-    sent_f = send(1, (xs_f, xr_f, *rows), (zs_f, zr_f, *corners), (ys_f, yr_f, *sides))
+    sent_t = send(0, (zs_bf, zr_bf, *corners), (ys_bf, yr_bf, *sides), (xs_t, xr_t, *rows))
+    sent_f = send(1, (zs_f, zr_f, *corners), (ys_f, yr_f, *sides), (xs_f, xr_f, *rows))
+    sent_bf = send(4, (xs_bf, xr_bf, *rows))
 
     for device in near:
         pl.semaphore_signal(hello.at[0], inc=1, device_id=device, device_id_type=MESH)
@@ -291,14 +294,14 @@
     def corner_f(recv):
         return [[jnp.where(sub1 < 4, recv[2 + side], recv[side])] for side in range(2)]
 
-    arrived(sent_bf)
+    arrived(sent_t)
 
     def rim_trans(s, old):
         at = pl.ds(s * PACK, PACK)
-        tx[1, at] = get_rows(xr_bf, 8, s)
-        fy = get_rows(xr_bf, 9, s)
+        tx[1, at] = get_rows(xr_t, 0, s)
+        fy = get_rows(xr_t, 1, s)
         ty[1, at] = fy
-        tz[1, at] = get_rows(xr_bf, 10, s)
+        tz[1, at] = get_rows(xr_t, 2, s)
         for t in range(PACK):
             old = pack_cols(old, fy[t], s * PACK + t)
         return old
@@ -325,52 +328,61 @@
     def ends(packed, s):
         return jnp.stack([pltpu.roll(packed, 125 - WIDE * (s * CHUNK + t), 1) for t in range(CHUNK)])
 
-    def faces_late(s, cols):
-        cols = [list(c) for c in cols]
-        at4 = pl.ds(s * PACK, PACK)
-        rim_mob = [get_rows(xr_bf, k, s) for k in range(4)]
-        rim_acc = [get_rows(xr_bf, 4 + k, s) for k in range(4)]
-        rim_grad = [get_rows(xr_f, c, s) for c in range(2)]
+    def late_system(block, cols, step, acc, mob, grad, faces):
+        at = pl.ds(step * CHUNK, CHUNK)
+        inv, mat = block_system(acc, mob, faces)
+        for k in range(4):
+            k_late[block, k, at] = mat[k]
+        first = transpose_apply(inv, grad)
+        for c in range(2):
+            base_late[block, c, at] = first[c]
+            y_a[block, c, pl.ds(step * CHUNK + 1, CHUNK)] = first[c]
+            for t in range(CHUNK):
+                cols[c] = pack_cols(cols[c], first[c][t], step * CHUNK + t)
+
+    def own_systems(step, cols):
+        cols = list(cols)
+        at = pl.ds(step * CHUNK, CHUNK)
+        after = pl.ds(step * CHUNK + 1, CHUNK)
+        lane = iota((CHUNK, 8, 128), 2)
+        far_x = row_shift(tx[0, at], tx[1, at], 7)
+        acc = [accum[k, at].astype(F32) for k in range(4)]
+        for block in range(2):
+            fy = ty[block, at]
+            far_y = pltpu.roll(jnp.where(lane == 0, ends(rim_ty[block], step), fy), 127, 2)
+            txp[block, at] = far_x[block]
+            typ[block, at] = far_y
+            if block == 0:
+                faces = tx[block, at] + far_x[block] + fy + far_y + tz[block, at] + tz[block, after]
+                mob = [mob_late[k, at].astype(F32) for k in range(4)]
+                late_system(0, cols, step, acc, mob, [grad_late[c, at] for c in range(2)], faces)
+                inv, mat = block_system(acc, [mob_early[k, at].astype(F32) for k in range(4)], faces)
+                for k in range(4):
+                    k_early[0, k, at] = mat[k]
+                    inv_early[k, at] = inv[k]
+        return tuple(cols)
+
+    late_own = lax.fori_loop(0, steps, own_systems, (zero, zero), unroll=5)
+
+    def rim_systems(s, cols):
+        cols = list(cols)
+        mob = [get_rows(xr_bf, k, s) for k in range(4)]
+        acc = [get_rows(xr_bf, 4 + k, s) for k in range(4)]
+        grad = [get_rows(xr_f, c, s) for c in range(2)]
         for h in range(PACK // CHUNK):
             part = slice(h * CHUNK, (h + 1) * CHUNK)
             step = s * (PACK // CHUNK) + h
             at = pl.ds(step * CHUNK, CHUNK)
             after = pl.ds(step * CHUNK + 1, CHUNK)
-            lane = iota((CHUNK, 8, 128), 2)
-            far_x = row_shift(tx[0, at], tx[1, at], 7)
-            for block in range(2):
-                fy = ty[block, at]
-                far_y = pltpu.roll(jnp.where(lane == 0, ends(rim_ty[block], step), fy), 127, 2)
-                txp[block, at] = far_x[block]
-                typ[block, at] = far_y
-                faces = tx[block, at] + far_x[block] + fy + far_y + tz[block, at] + tz[block, after]
-                if block == 0:
-                    mob = [mob_late[k, at].astype(F32) for k in range(4)]
-                    acc = [accum[k, at].astype(F32) for k in range(4)]
-                    grad = [grad_late[c, at] for c in range(2)]
-                else:
-                    mob, acc, grad = ([x[part] for x in f] for f in (rim_mob, rim_acc, rim_grad))
-                inv, mat = block_system(acc, mob, faces)
-                for k in range(4):
-                    k_late[block, k, at] = mat[k]
-                first = transpose_apply(inv, grad)
-                for c in range(2):
-                    base_late[block, c, at] = first[c]
-                    y_a[block, c, after] = first[c]
-                    for t in range(CHUNK):
-                        cols[block][c] = pack_cols(cols[block][c], first[c][t], step * CHUNK + t)
-                if block == 0:
-                    mob = [mob_early[k, at].astype(F32) for k in range(4)]
-                    inv, mat = block_system(acc, mob, faces)
-                    for k in range(4):
-                        k_early[0, k, at] = mat[k]
-                        inv_early[k, at] = inv[k]
-        return tuple(tuple(c) for c in cols)
-
+            faces = tx[1, at] + txp[1, at] + ty[1, at] + typ[1, at] + tz[1, at] + tz[1, after]
+            late_system(1, cols, step, *([x[part] for x in f] for f in (acc, mob, grad)), faces)
+        return tuple(cols)
+
+    cols_none = ((zero, zero), (zero, zero))
     arrived(sent_f)
-    sent_me = send(2, (xs_me, xr_me, *rows), (ys_me, yr_me, *sides))
-    cols_none = ((zero, zero), (zero, zero))
-    late_cols = lax.fori_loop(0, packs, faces_late, cols_none, unroll=5)
+    arrived(sent_bf)
+    sent_me = send(2, (ys_me, yr_me, *sides), (xs_me, xr_me, *rows))
+    late_cols = (late_own, lax.fori_loop(0, packs, rim_systems, (zero, zero), unroll=5))
     rim_mob_y, rim_acc_y = rim_bf[0:4], rim_bf[4:8]
     rim_grad_y = rim_fields([[yr_f[side]] for side in range(2)], corner_f(zr_f))
     for block in range(2):
@@ -477,7 +489,7 @@
         ys_e[side] = pair[side]
         for end in range(2):
             zs_e[2 * end + side] = pair[side]
-    sent_e = send(3, (xs_e, xr_e, *rows), (zs_e, zr_e, *corners), (ys_e, yr_e, *sides))
+    sent_e = send(3, (zs_e, zr_e, *corners), (ys_e, yr_e, *sides), (xs_e, xr_e, *rows))
 
     pl.semaphore_wait(hello.at[0], len(near))
     for device in far:
@@ -511,12 +523,12 @@
         terms = onehot_dot(cell_row[...], lines) * col_weight[...]
         return jnp.sum(terms, axis=1, keepdims=True)
 
-    own_lane = lane_p - wells % 8
+    own_lane = lane_p - 8 * group * (wells // 8 % group) - wells % 8
     spread = jnp.zeros((256, 128), F32)
     for c in range(2):
         spread = jnp.where(own_lane == 8 * (c + 2), picked(y_b[0, c, pl.ds(1, nz)]), spread)
     owner = jnp.where(
-        iota((n_gx, 256), 0) == jnp.broadcast_to(perf_well[0] // 8, (n_gx, 256)), 1.0, 0.0
+        iota((planes, 256), 0) == jnp.broadcast_to(perf_well[0] // (8 * group), (planes, 256)), 1.0, 0.0
     ).astype(BF16)
 
     arrived(sent_e)
@@ -553,63 +565,48 @@
     for c in range(2):
         spread = jnp.where(own_lane == 8 * c, picked(early_out[c]), spread)
     partial = onehot_dot(owner, spread)
-    for o in range(n_gx):
+    for o in range(planes):
         pbuf[o] = partial[o : o + 1]
 
-    for d in range(a_count - 1):
-        t, device = a_partner(d)
+    pl.semaphore_wait(hello.at[1], len(far))
+    for d in range(planes - 1):
+        to = d + (d >= plane).astype(jnp.int32)
+        place = plane - (plane > to).astype(jnp.int32)
         copy = pltpu.make_async_remote_copy(
-            src_ref=pbuf.at[pl.ds(t * per_dev, per_dev)], dst_ref=ra.at[pl.ds(d * per_dev, per_dev)],
-            send_sem=a_send.at[d], recv_sem=a_recv, device_id=device, device_id_type=MESH,
+            src_ref=pbuf.at[to], dst_ref=ra.at[place],
+            send_sem=a_send.at[d], recv_sem=a_recv, device_id=(to * group + spot, j), device_id_type=MESH,
         )
         copy.start()
         started.append(copy)
-    landed = ra.at[pl.ds(0, n_gx - per_dev)]
-    pltpu.make_async_copy(landed, landed, a_recv).wait()
-    for r in range(per_dev):
-        total = pbuf[q * per_dev + r]
-        for d in range(a_count - 1):
-            total = total + ra[d * per_dev + r]
-        sb[r] = total
-
-    pl.semaphore_wait(hello.at[1], len(far))
-
-    def b_copy(r, dest_j):
-        dest_i = q * per_dev + r
-        own = jnp.logical_and(dest_i == i, j == dest_j)
-        return own, pltpu.make_async_remote_copy(
-            src_ref=sb.at[r], dst_ref=rb.at[plane], send_sem=b_send.at[r * n_gy + dest_j], recv_sem=b_recv,
-            device_id=(dest_i, dest_j), device_id_type=MESH,
+    pltpu.make_async_copy(ra, ra, a_recv).wait()
+    total = pbuf[plane]
+    for d in range(planes - 1):
+        total = total + ra[d]
+    sb[...] = total
+
+    for d, device in enumerate(plane_partners):
+        copy = pltpu.make_async_remote_copy(
+            src_ref=sb, dst_ref=rb.at[d], send_sem=b_send.at[d], recv_sem=b_recv,
+            device_id=device, device_id_type=MESH,
         )
-
-    for r in range(per_dev):
-        for dest_j in range(n_gy):
-            own, copy = b_copy(r, dest_j)
-            pl.when(jnp.logical_not(own))(copy.start)
-            pl.when(own)(pltpu.make_async_copy(sb.at[r], rb.at[plane], b_recv).start)
+        copy.start()
+        started.append(copy)
+    for copy in started:
+        copy.wait_send()
     pltpu.make_async_copy(rb, rb, b_recv).wait()
-    total = rb[0]
-    for p in range(1, planes):
-        total = total + rb[p]
-    total = jnp.broadcast_to(total, (8, 128))
+    for d in range(len(offsets)):
+        total = total + rb[d]
+    total = pltpu.roll(jnp.broadcast_to(total, (8, 128)), 128 - 8 * group * spot, 1)
     out = total
     for k in range(1, 4):
         out = jnp.where(sub1 == k, pltpu.roll(total, 128 - 8 * k, 1), out)
     wells_out[...] = out[0:4, 0:8]
 
-    for copy in started:
-        copy.wait_send()
-    for r in range(per_dev):
-        for dest_j in range(n_gy):
-            own, copy = b_copy(r, dest_j)
-            pl.when(jnp.logical_not(own))(copy.wait_send)
-
 
 def per_device(n_gx, n_gy, *args):
     nz = args[5].shape[0]
-    a_count = 4 * n_gy
-    per_dev = n_gx // a_count
     planes = n_gx // 4
+    others = 4 * n_gy - 1
     packs = nz // PACK
 
     def f32(*lead):
@@ -634,18 +631,18 @@
             f32(2, 4, nz), f32(2, 4, nz), f32(4, nz), f32(2, 2, nz), f32(2, 2, nz),
             f32(2, 2, nz + 2), f32(2, 2, nz + 2),
             f32(6, 2), f32(2, 4), f32(2, 4), f32(2, 2), f32(2, 2), f32(2, 2), f32(2, 2),
-            bf16(2, 11, packs), f32(2, 2, 2 * packs), bf16(2, 4, packs), f32(2, 2, 2 * packs),
-            bf16(2, 11, packs), f32(2, 2, 2 * packs), bf16(2, 4, packs), f32(2, 2, 2 * packs),
-            dma((4, 2)), dma((4, 2)),
+            bf16(2, 3, packs), bf16(2, 8, packs), f32(2, 2, 2 * packs), bf16(2, 4, packs), f32(2, 2, 2 * packs),
+            bf16(2, 3, packs), bf16(2, 8, packs), f32(2, 2, 2 * packs), bf16(2, 4, packs), f32(2, 2, 2 * packs),
+            dma((5, 2)), dma((5, 2)),
             bf16(2, 3), f32(2), bf16(2), f32(2),
             bf16(2, 3), f32(2), bf16(2), f32(2),
             dma((4, 2)), dma((4, 2)),
             bf16(4, 2), f32(4), f32(4), bf16(4, 2), f32(4), f32(4),
             dma((4, 4)), dma((4, 4)),
             pltpu.VMEM((256, 256), BF16), pltpu.VMEM((256, 128), F32),
-            pltpu.VMEM((n_gx, 1, 128), F32), pltpu.VMEM((n_gx, 1, 128), F32),
-            pltpu.VMEM((per_dev, 1, 128), F32), pltpu.VMEM((planes, 1, 128), F32),
-            dma((a_count,)), dma, dma((per_dev * n_gy,)), dma,
+            pltpu.VMEM((planes, 1, 128), F32), pltpu.VMEM((planes - 1, 1, 128), F32),
+            pltpu.VMEM((1, 128), F32), pltpu.VMEM((others, 1, 128), F32),
+            dma((planes - 1,)), dma, dma((others,)), dma,
             pltpu.SemaphoreType.REGULAR((2,)),
         ],
         compiler_params=pltpu.CompilerParams(

time: 52.4 us -> 49.7 us (0.948)
  Pallas kernels: 50.4 us -> 47.6 us
    pallas_call x1, Pallas kernels: 50.4 us -> 47.6 us  [per_device(): pl.pallas_call(functools.partial(kernel, n_gx, n_gy, nz), out_shape=(pltp...]
where the time goes in v6:
time: 49.7 us; the launch traced here: 49.5 us
  Pallas kernels  47.6 us (96%)
  local copies, waits for them, and re-layouts  1.25 us (3%)
  between operations  0.64 us (1%)
    pallas_call x1, Pallas kernels, per_device(): pl.pallas_call(functools.partial(kernel, n_gx, n_gy, nz), out_shape=(pltp...  47.6 us
    unnamed x2, local copies, waits for them, and re-layouts  1.25 us

profile of v6, /device:TPU:1, one launch (start us, length us, event | category | flops | bytes accessed | tf_op | source)
XLA Modules:
  0.0 49.5 jit_solution(8825487342762949645)
XLA Ops:
  0.6 47.6 %shard_map.122 = (f32[2,20,8,128]{3,2,1,0:T(8,128)S(1)}, f32[4,8]{1,0:T(4,128)S(1)}) custom-call(f32[2,20,8,128]{3,2,1,0:T(8,128)} %refs_0_.1, f32[2,20,8,128]{3,2,1,0:T(8,128)} %refs_1_.1, bf16[4,20,8,128]{3,2,1,0:T(8,128)(2,1)} %refs_2_.1, bf16[4,20,8,128]{3,2,1,0:T(8,128)(2,1)} %refs_3_.1, bf16[4,20,8,128]{3,2,1,0:T(8,128)(2,1)} %refs_4_.1, ...), custom_call_target="tpu_custom_call" | custom-call | tf_op jit(solution)/shard_map/pallas_call | solution.py:620
  48.3 0.7 %copy.15 = f32[2,20,8,128]{3,2,1,0:T(8,128)} copy(f32[2,20,8,128]{3,2,1,0:T(8,128)S(1)} %get-tuple-element.2) | data formatting | bytes 327680
  48.9 0.6 %copy.16 = f32[4,8]{1,0:T(4,128)} copy(f32[4,8]{1,0:T(4,128)S(1)} %get-tuple-element.3) | data formatting | bytes 256

commit v7 on v6

--- a/solution.py
+++ b/solution.py
@@ -11,7 +11,7 @@
 F32 = jnp.float32
 BF16 = jnp.bfloat16
 PACK = 4
-CHUNK = 2
+CHUNK = 4
 WIDE = 6
 
 
@@ -381,6 +381,9 @@
     cols_none = ((zero, zero), (zero, zero))
     arrived(sent_f)
     arrived(sent_bf)
+    pl.semaphore_wait(hello.at[0], len(near))
+    for device in far:
+        pl.semaphore_signal(hello.at[1], inc=1, device_id=device, device_id_type=MESH)
     sent_me = send(2, (ys_me, yr_me, *sides), (xs_me, xr_me, *rows))
     late_cols = (late_own, lax.fori_loop(0, packs, rim_systems, (zero, zero), unroll=5))
     rim_mob_y, rim_acc_y = rim_bf[0:4], rim_bf[4:8]
@@ -491,9 +494,6 @@
             zs_e[2 * end + side] = pair[side]
     sent_e = send(3, (zs_e, zr_e, *corners), (ys_e, yr_e, *sides), (xs_e, xr_e, *rows))
 
-    pl.semaphore_wait(hello.at[0], len(near))
-    for device in far:
-        pl.semaphore_signal(hello.at[1], inc=1, device_id=device, device_id_type=MESH)
     arrived(sent_me)
 
     def rim_early_mats(s, _):
@@ -569,9 +569,9 @@
         pbuf[o] = partial[o : o + 1]
 
     pl.semaphore_wait(hello.at[1], len(far))
-    for d in range(planes - 1):
-        to = d + (d >= plane).astype(jnp.int32)
-        place = plane - (plane > to).astype(jnp.int32)
+    farthest = sorted(range(1, planes), key=lambda o: -min(o, planes - o))
+    for d, offset in enumerate(farthest):
+        to, place = (plane + offset) % planes, d
         copy = pltpu.make_async_remote_copy(
             src_ref=pbuf.at[to], dst_ref=ra.at[place],
             send_sem=a_send.at[d], recv_sem=a_recv, device_id=(to * group + spot, j), device_id_type=MESH,

time: 49.7 us -> 49.5 us (level)
  no operation moved by 1% of the time
where the time goes in v7:
time: 49.5 us; the launch traced here: 49.4 us
  Pallas kernels  47.5 us (96%)
  local copies, waits for them, and re-layouts  1.25 us (3%)
  between operations  0.64 us (1%)
    pallas_call x1, Pallas kernels, per_device(): pl.pallas_call(functools.partial(kernel, n_gx, n_gy, nz), out_shape=(pltp...  47.5 us
    unnamed x2, local copies, waits for them, and re-layouts  1.25 us

profile of v7, /device:TPU:1, one launch (start us, length us, event | category | flops | bytes accessed | tf_op | source)
XLA Modules:
  0.0 49.4 jit_solution(6633646732030474293)
XLA Ops:
  0.6 47.5 %shard_map.122 = (f32[2,20,8,128]{3,2,1,0:T(8,128)S(1)}, f32[4,8]{1,0:T(4,128)S(1)}) custom-call(f32[2,20,8,128]{3,2,1,0:T(8,128)} %refs_0_.1, f32[2,20,8,128]{3,2,1,0:T(8,128)} %refs_1_.1, bf16[4,20,8,128]{3,2,1,0:T(8,128)(2,1)} %refs_2_.1, bf16[4,20,8,128]{3,2,1,0:T(8,128)(2,1)} %refs_3_.1, bf16[4,20,8,128]{3,2,1,0:T(8,128)(2,1)} %refs_4_.1, ...), custom_call_target="tpu_custom_call" | custom-call | tf_op jit(solution)/shard_map/pallas_call | solution.py:620
  48.2 0.7 %copy.15 = f32[2,20,8,128]{3,2,1,0:T(8,128)} copy(f32[2,20,8,128]{3,2,1,0:T(8,128)S(1)} %get-tuple-element.2) | data formatting | bytes 327680
  48.8 0.6 %copy.16 = f32[4,8]{1,0:T(4,128)} copy(f32[4,8]{1,0:T(4,128)S(1)} %get-tuple-element.3) | data formatting | bytes 256
